TPU v7x, 256 devices: a whole 4x4x8 slice. The times are simulated.
256 devices in a mesh: src: 16 (over z_lo, y, core), rcv: 16 (over x, z_hi).
Axes of the slice: x: 4, y: 4, z: 8 (z_hi: 4, z_lo: 2; z = z_hi * 2 + z_lo), core: 2. Of those that a mesh axis runs over, the one named last changes fastest.
Arguments:
- traces: bfloat16 [512, 512, 512], P('src', 'rcv'), may hold values from -6 to 6
- dead_mask: int32 [512, 512], P('src', 'rcv'), may hold values 0 or 1
- filters: bfloat16 [512, 256], P(('src', 'rcv')), may hold values from -0.375 to 0.375
- station_of_slot: int32 [512], replicated, may hold values from 0 to 511, each once
Outputs:
- residual: bfloat16 [512, 512, 512], P('src', 'rcv')
- grad_receiver: float32 [512, 256], P('rcv')
- grad_source: float32 [512, 256], P('src')
Inputs may be any that keep to these rules, and one draw needn't show every extreme that they name: `station_of_slot`: every station number stands in exactly one slot. `dead_mask`: 1 marks a live trace, 0 a dead one.
All inputs are finite; a program needn't handle non-finite values. No bound on the sum of `dead_mask` on one device may be relied on, other than what follows from the above.
Results may differ from a plain program's by a relative error of at most 0.014.
Values may be sent and summed in bfloat16 or wider, within the bound.
A program may use at most 64 MiB of HBM per device.

v0:
```python
import math

import jax
import jax.numpy as jnp
from jax import lax
from jax.sharding import PartitionSpec as P

station_group = 4


def toeplitz_tables(tap_rows, trace_len):
    group_count, tap_count = tap_rows.shape
    period = trace_len + tap_count
    padded = jnp.concatenate(
        [tap_rows, jnp.zeros((group_count, period - tap_count), tap_rows.dtype)], axis=1
    )
    tiled = jnp.tile(padded, (1, trace_len))[:, : trace_len * (period - 1)]
    return tiled.reshape(group_count, trace_len, period - 1)[:, :, :trace_len]


def convolve(lead_traces, tap_rows):
    lead_count, row_count, trace_len = lead_traces.shape
    group_total = lead_count // station_group

    def filter_group(inputs_pair):
        trace_block, block_taps = inputs_pair
        tables = toeplitz_tables(block_taps, trace_len)
        return jnp.einsum(
            "gpu,gut->gpt", trace_block, tables, preferred_element_type=jnp.float32
        ).astype(jnp.bfloat16)

    grouped = lead_traces.reshape(group_total, station_group, row_count, trace_len)
    grouped_taps = tap_rows.reshape(group_total, station_group, tap_rows.shape[1])
    return lax.map(filter_group, (grouped, grouped_taps)).reshape(lead_count, row_count, trace_len)


def correlate(lead_residual, lead_traces, tap_count):
    lead_count, row_count, trace_len = lead_traces.shape
    group_total = lead_count // station_group
    block_len = min(128, trace_len)

    def lag_group(inputs_pair):
        residual_block, trace_block = inputs_pair
        delayed = jnp.pad(trace_block, ((0, 0), (0, 0), (tap_count, 0)))
        accumulated = jnp.zeros((station_group, tap_count), jnp.float32)
        for begin_at in range(0, trace_len, block_len):
            products = jnp.einsum(
                "gpa,gpj->gaj",
                residual_block[:, :, begin_at : begin_at + block_len],
                delayed[:, :, begin_at : begin_at + block_len + tap_count],
                preferred_element_type=jnp.float32,
            )
            flattened = products.reshape(station_group, block_len * (block_len + tap_count))
            flattened = jnp.concatenate(
                [flattened, jnp.zeros((station_group, block_len), jnp.float32)], axis=1
            )
            skewed = flattened.reshape(station_group, block_len, block_len + tap_count + 1)
            accumulated = accumulated + jnp.sum(skewed[:, :, 1 : tap_count + 1], axis=1)
        return accumulated[:, ::-1]

    grouped_residual = lead_residual.reshape(group_total, station_group, row_count, trace_len)
    grouped_traces = lead_traces.reshape(group_total, station_group, row_count, trace_len)
    return lax.map(lag_group, (grouped_residual, grouped_traces)).reshape(lead_count, tap_count)


def shards(traces, dead_mask, filters, station_of_slot):
    src_rows, rcv_cols, trace_len = traces.shape
    tap_count = filters.shape[1]
    src_count = lax.axis_size("src")
    rcv_count = lax.axis_size("rcv")
    fine_size = src_rows // rcv_count
    filter_table = lax.all_gather(filters, ("src", "rcv"), axis=0, tiled=True)
    local_rows = jnp.arange(src_rows, dtype=jnp.int32)
    local_cols = jnp.arange(rcv_cols, dtype=jnp.int32)
    row_slots = lax.axis_index("src") * src_rows + local_rows
    col_slots = (
        local_cols // fine_size * rcv_count + lax.axis_index("rcv")
    ) * fine_size + local_cols % fine_size
    row_taps = filter_table[station_of_slot[row_slots]]
    col_taps = filter_table[station_of_slot[col_slots]]
    blocks = traces.reshape(rcv_count, fine_size, src_count, fine_size, trace_len)
    moved = lax.all_to_all(
        lax.all_to_all(blocks, "src", split_axis=2, concat_axis=2, tiled=True),
        "rcv",
        split_axis=0,
        concat_axis=0,
        tiled=True,
    )
    mirrored = moved.transpose(0, 3, 2, 1, 4).reshape(src_rows, rcv_cols, trace_len)
    by_column = jnp.transpose(traces, (1, 0, 2))
    column_filtered = convolve(by_column, col_taps)
    row_filtered = convolve(mirrored, row_taps)
    live = dead_mask.astype(jnp.float32)[:, :, None]
    residual = (
        live
        * (
            jnp.transpose(column_filtered, (1, 0, 2)).astype(jnp.float32)
            - row_filtered.astype(jnp.float32)
        )
    ).astype(jnp.bfloat16)
    scale = 1.0 / math.sqrt(src_rows * src_count * trace_len)
    receiver_terms = correlate(jnp.transpose(residual, (1, 0, 2)), by_column, tap_count) * scale
    source_terms = correlate(residual, mirrored, tap_count) * -scale
    grad_receiver = lax.psum(receiver_terms.astype(jnp.bfloat16), "src").astype(jnp.float32)
    grad_source = lax.psum(source_terms.astype(jnp.bfloat16), "rcv").astype(jnp.float32)
    return (residual, grad_receiver, grad_source)


def solution(mesh):
    placed = (P("src", "rcv", None), P("src", "rcv"), P(("src", "rcv"), None), P())
    return jax.shard_map(
        shards,
        mesh=mesh,
        in_specs=placed,
        out_specs=(P("src", "rcv", None), P("rcv", None), P("src", None)),
        check_vma=False,
    )
```

profile of v0, /device:TPU:1, one launch (start us, length us, event | category | flops | bytes accessed | tf_op | source)
XLA Modules:
  0.0 1349.8 jit_solution(13184457851218151056)
XLA Ops:
  4.7 7.3 all-to-all-start
  12.1 607.3 %all-gather = bf16[256,2,256]{2,1,0:T(2,128)(2,1)S(1)} all-gather(bf16[1,2,256]{2,1,0:T(2,128)(2,1)S(1)} %bitcast.163), channel_id=1, replica_groups=mesh['src'=16,'rcv'=16] {'src','rcv'}, dimensions={0}, use_global_device_ids=true | all-gather | bytes 263168 | tf_op jit(solution)/shard_map/all_gather | solution.py:72
  624.5 7.2 all-to-all-start.1
  632.8 139.8 %while.44 = (s32[]{:T(128)}, bf16[8,4,32,512]{3,2,1,0:T(8,128)(2,1)}, bf16[8,4,32,512]{3,2,1,0:T(8,128)(2,1)}, bf16[8,4,256]{2,1,0:T(4,128)(2,1)S(1)}, s32[]{:T(128)}, /*index=5*/bf16[]{:T(256)}) while((s32[]{:T(128)}, bf16[8,4,32,512]{3,2,1,0:T(8,128)(2,1)}, bf16[8,4,32,512]{3,2,1,0:T(8,128)(2,1)}, bf16[8,4,256]{2,1,0:T(4,128)(2,1)S(1)}, ...), condition=%wide.region_1.2_spmd, body=%wide.region_0.1_spmd.sunk | while | flops 67174400 | bytes 30665804 | solution.py:34
  636.6 2.8 reshape.320
  639.4 8.8 reshape.321
  654.1 2.8 reshape.320
  656.9 8.8 reshape.321
  671.5 2.8 reshape.320
  674.4 8.8 reshape.321
  689.0 2.8 reshape.320
  691.8 8.8 reshape.321
  706.5 2.8 reshape.320
  709.3 8.8 reshape.321
  726.8 8.8 reshape.321
  744.3 8.8 reshape.321
  761.8 8.8 reshape.321
  774.0 2.9 bitcast_convert_fusion
  781.4 140.3 %while.45 = (s32[]{:T(128)}, bf16[8,4,32,512]{3,2,1,0:T(8,128)(2,1)}, bf16[8,4,32,512]{3,2,1,0:T(8,128)(2,1)}, bf16[8,4,256]{2,1,0:T(4,128)(2,1)S(1)}, s32[]{:T(128)}, /*index=5*/bf16[]{:T(256)}) while((s32[]{:T(128)}, bf16[8,4,32,512]{3,2,1,0:T(8,128)(2,1)}, bf16[8,4,32,512]{3,2,1,0:T(8,128)(2,1)}, bf16[8,4,256]{2,1,0:T(4,128)(2,1)S(1)}, ...), condition=%wide.region_3.4_spmd, body=%wide.region_2.3_spmd.sunk | while | flops 67174400 | bytes 30665804 | solution.py:34
  788.6 8.8 reshape.323
  806.1 8.8 reshape.323
  823.6 8.8 reshape.323
  841.0 8.8 reshape.323
  858.5 8.8 reshape.323
  876.0 8.8 reshape.323
  893.5 8.8 reshape.323
  910.9 8.8 reshape.323
  921.8 3.1 fusion.45
  924.8 80.1 %while.47 = (s32[]{:T(128)}, f32[8,4,256]{2,1,0:T(4,128)S(1)}, bf16[8,4,32,512]{3,2,1,0:T(8,128)(2,1)S(1)}, bf16[8,4,32,512]{3,2,1,0:T(8,128)(2,1)}, s32[]{:T(128)}, /*index=5*/f32[]{:T(128)}) while((s32[]{:T(128)}, f32[8,4,256]{2,1,0:T(4,128)S(1)}, bf16[8,4,32,512]{3,2,1,0:T(8,128)(2,1)S(1)}, bf16[8,4,32,512]{3,2,1,0:T(8,128)(2,1)}, ...), condition=%wide.region_16.17_spmd, body=%wide.region_11.16_spmd.sunk | while | flops 50854912 | bytes 25309276 | solution.py:63
  1005.0 68.7 %psum.15 = bf16[32,256]{1,0:T(8,128)(2,1)S(1)} all-reduce(bf16[32,256]{1,0:T(8,128)(2,1)S(1)} %convert_element_type.63), channel_id=1, replica_groups=mesh['src'=16,'rcv'=16] {'rcv'}, use_global_device_ids=true, to_apply=%region_17.18 | all-reduce | flops 8192 | bytes 32768 | tf_op jit(solution)/shard_map/psum | solution.py:105
  1074.9 79.9 %while.46 = (s32[]{:T(128)}, f32[8,4,256]{2,1,0:T(4,128)S(1)}, bf16[8,4,32,512]{3,2,1,0:T(8,128)(2,1)S(1)}, bf16[8,4,32,512]{3,2,1,0:T(8,128)(2,1)}, s32[]{:T(128)}, /*index=5*/f32[]{:T(128)}) while((s32[]{:T(128)}, f32[8,4,256]{2,1,0:T(4,128)S(1)}, bf16[8,4,32,512]{3,2,1,0:T(8,128)(2,1)S(1)}, bf16[8,4,32,512]{3,2,1,0:T(8,128)(2,1)}, ...), condition=%wide.region_9.10_spmd, body=%wide.region_4.9_spmd.sunk | while | flops 50854912 | bytes 25309276 | solution.py:63
  1154.8 194.1 %psum.14 = bf16[32,256]{1,0:T(8,128)(2,1)S(1)} all-reduce(bf16[32,256]{1,0:T(8,128)(2,1)S(1)} %convert_element_type.60), channel_id=1, replica_groups=mesh['src'=16,'rcv'=16] {'src'}, use_global_device_ids=true, to_apply=%region_10.11 | all-reduce | flops 8192 | bytes 32768 | tf_op jit(solution)/shard_map/psum | solution.py:104
  (538 shorter events, 300.3 us)
Async XLA Ops:
  0.6 618.9 %copy-start = (s32[512]{0:T(512)S(1)}, s32[512]{0:T(512)}, u32[]{:S(2)}) copy-start(s32[512]{0:T(512)} %param.15) | copy-start | bytes 6148
  0.6 11.4 copy-start.5
  2.1 618.7 %copy-start.3 = (bf16[32,32,512]{2,1,0:T(8,128)(2,1)S(1)}, bf16[32,32,512]{2,1,0:T(8,128)(2,1)}, u32[]{:S(2)}) copy-start(bf16[32,32,512]{2,1,0:T(8,128)(2,1)} %param.12) | copy-start | bytes 3145732
  4.7 617.7 %all-to-all-start = ((bf16[16,2,16,2,512]{4,1,3,0,2:T(2,128)(2,1)}), bf16[16,2,16,2,512]{4,1,3,0,2:T(2,128)(2,1)S(1)}, u32[]{:S(2)}, u32[]{:S(2)}) async-start(bf16[16,2,16,2,512]{4,1,3,0,2:T(2,128)(2,1)} %copy.25), calls=%async_computation | async-start | bytes 2097152 | tf_op jit(solution)/shard_map/all_to_all | solution.py:83
  624.5 152.4 %all-to-all-start.1 = ((bf16[16,2,16,2,512]{4,1,3,2,0:T(2,128)(2,1)}), bf16[16,2,16,2,512]{4,1,3,2,0:T(2,128)(2,1)}, u32[]{:S(2)}, u32[]{:S(2)}) async-start(bf16[16,2,16,2,512]{4,1,3,2,0:T(2,128)(2,1)} %copy.26), calls=%async_computation.1 | async-start | bytes 2097152 | tf_op jit(solution)/shard_map/all_to_all | solution.py:82
  632.7 141.2 %copy-start.4 = (s32[32,32]{1,0:T(8,128)S(1)}, s32[32,32]{1,0:T(8,128)}, u32[]{:S(2)}) copy-start(s32[32,32]{1,0:T(8,128)} %param.13) | copy-start | bytes 12292
  1005.0 69.9 %copy-start.2 = (bf16[8,4,32,512]{3,2,1,0:T(8,128)(2,1)}, bf16[8,4,32,512]{3,2,1,0:T(8,128)(2,1)S(1)}, u32[]{:S(2)}) copy-start(bf16[8,4,32,512]{3,2,1,0:T(8,128)(2,1)S(1)} %get-tuple-element.393) | copy-start | bytes 3145732
  1154.8 194.7 %copy-start.1 = (s32[512]{0:T(512)S(1)}, s32[512]{0:T(512)}, u32[]{:S(2)}) copy-start(s32[512]{0:T(512)} %param.15) | copy-start | bytes 6148
where the time goes:
time: 1370 us; the launch traced here: 1350 us
  blocking collectives  870 us (64%)
  local copies, waits for them, and re-layouts  388 us (28%)
  matrix products  51.5 us (4%)
  other arithmetic  21.3 us (2%)
  starting transfers between devices  14.5 us (1%)
    all_gather x1, blocking collectives, shards(): filter_table = lax.all_gather(filters, ('src', 'rcv'), axis=0, tiled=True)  607 us
    psum x1, blocking collectives, shards(): lax.psum(receiver_terms.astype(jnp.bfloat16), 'src').astype(jnp.float32)  194 us
    reshape x16, local copies, waits for them, and re-layouts, toeplitz_tables(): return tiled.reshape(group_count, trace_len, period - 1)[:, :, :trace_len]  140 us
    while x112, local copies, waits for them, and re-layouts  120 us
    psum x1, blocking collectives, shards(): lax.psum(source_terms.astype(jnp.bfloat16), 'rcv').astype(jnp.float32)  68.7 us
    reshape x64, local copies, waits for them, and re-layouts, lag_group(): flattened.reshape(station_group, block_len, block_len + tap_count + 1)  65 us
    dot_general x16, matrix products, filter_group(): jnp.einsum('gpu,gut->gpt', trace_block, tables, preferred_element_type=jn...  32.4 us
  transfers between devices with their start and end apart: 2, of which 0 were waited for; matrix products, arithmetic and copies ran while one was open for 11% of the time, Pallas kernels for 0%

commit v1 on v0

--- a/solution.py
+++ b/solution.py
@@ -1,11 +1,187 @@
+import functools
 import math
 
 import jax
 import jax.numpy as jnp
 from jax import lax
+from jax.experimental import pallas as pl
+from jax.experimental.pallas import tpu as pltpu
 from jax.sharding import PartitionSpec as P
 
+MESH = pl.DeviceIdType.MESH
 station_group = 4
+
+
+def digits_of(n_src, n_rcv):
+    if (n_src, n_rcv) == (16, 16):
+        return (2, 4, 2), (4, 4)
+    return (1, n_src // 2, 2), (n_rcv // 2, 2)
+
+
+def line_peers(S, R, n_src, n_rcv):
+    (nl, ny, nc), (nx, nh) = digits_of(n_src, n_rcv)
+    l, y, c = S // (ny * nc), lax.rem(S // nc, ny), lax.rem(S, nc)
+    x, h = R // nh, lax.rem(R, nh)
+
+    def at(dl, dy, dc, dx, dh):
+        s = (lax.rem(l + dl, nl) * ny + lax.rem(y + dy, ny)) * nc + lax.rem(c + dc, nc)
+        return s, lax.rem(x + dx, nx) * nh + lax.rem(h + dh, nh)
+
+    z = [at(a, 0, 0, 0, b) for a in range(nl) for b in range(nh) if a or b]
+    xs = [at(0, 0, 0, a, 0) for a in range(1, nx)]
+    ys = [at(0, a, 0, 0, 0) for a in range(1, ny)]
+    cs = [at(0, 0, a, 0, 0) for a in range(1, nc)]
+    return z, xs, ys, cs
+
+
+def enter(S, R, n_src, n_rcv, stage_sems):
+    z, xs, ys, cs = line_peers(S, R, n_src, n_rcv)
+    bar = pltpu.get_barrier_semaphore()
+    near = z + xs + ys + cs
+    for d in near:
+        pl.semaphore_signal(bar, inc=1, device_id=d, device_id_type=MESH)
+    pl.semaphore_wait(bar, len(near))
+    for i, group in enumerate((xs, ys, cs)):
+        for d in group:
+            pl.semaphore_signal(stage_sems.at[i], inc=1, device_id=d, device_id_type=MESH)
+        pl.semaphore_wait(stage_sems.at[i], len(group))
+
+
+def wait_bytes(ref, sem):
+    pltpu.make_async_copy(ref, ref, sem).wait()
+
+
+def exchange_kernel(n_src, n_rcv, x_ref, f_ref, recv, table, f_row, stage_sems, s_x, r_x, s_f, r_f, s_g, r_g):
+    S, R = lax.axis_index("src"), lax.axis_index("rcv")
+    enter(S, R, n_src, n_rcv, stage_sems)
+
+    def send_filter(j, c):
+        pltpu.make_async_remote_copy(
+            f_ref, f_row.at[R], s_f, r_f, device_id=(S, lax.rem(R + j, n_rcv)), device_id_type=MESH
+        ).start()
+        return c
+
+    lax.fori_loop(1, n_rcv, send_filter, 0)
+
+    def send_traces(i, c):
+        dS = lax.rem(S + i // n_rcv, n_src)
+        dR = lax.rem(R + lax.rem(i, n_rcv), n_rcv)
+        pltpu.make_async_remote_copy(
+            x_ref.at[dS, dR], recv.at[S, R], s_x, r_x.at[i // n_rcv], device_id=(dS, dR), device_id_type=MESH
+        ).start()
+        return c
+
+    lax.fori_loop(1, n_src * n_rcv, send_traces, 0)
+    f_row[R] = f_ref[...]
+    wait_bytes(f_row.at[pl.ds(0, n_rcv - 1)], r_f)
+    table[S] = f_row[...].astype(jnp.bfloat16).reshape(table.shape[1:])
+
+    def send_rows(k, c):
+        pltpu.make_async_remote_copy(
+            table.at[S], table.at[S], s_g, r_g, device_id=(lax.rem(S + k, n_src), R), device_id_type=MESH
+        ).start()
+        return c
+
+    lax.fori_loop(1, n_src, send_rows, 0)
+    recv[S, R] = x_ref[S, R]
+    wait_bytes(table.at[pl.ds(0, n_src - 1)], r_g)
+    for k in range(n_src):
+        wait_bytes(recv.at[0, pl.ds(0, n_rcv - (k == 0))], r_x.at[k])
+    wait_bytes(f_row.at[pl.ds(0, n_rcv - 1)], s_f)
+    wait_bytes(table.at[pl.ds(0, n_src - 1)], s_g)
+    for k in range(n_src):
+        wait_bytes(recv.at[0, pl.ds(0, n_rcv - (k == 0))], s_x)
+
+
+def exchange(tiles, own_filter):
+    n_src, n_rcv = tiles.shape[:2]
+    vm = pl.BlockSpec(memory_space=pltpu.VMEM)
+    D = pltpu.SemaphoreType.DMA
+    return pl.pallas_call(
+        functools.partial(exchange_kernel, n_src, n_rcv),
+        out_shape=(
+            jax.ShapeDtypeStruct(tiles.shape, tiles.dtype),
+            jax.ShapeDtypeStruct((n_src, n_rcv * 8, 128), jnp.bfloat16),
+        ),
+        in_specs=[vm, vm],
+        out_specs=(vm, vm),
+        scratch_shapes=[
+            pltpu.VMEM((n_rcv, 8, 128), jnp.float32),
+            pltpu.SemaphoreType.REGULAR((3,)),
+            D, D((n_src,)), D, D, D, D,
+        ],
+        compiler_params=pltpu.CompilerParams(
+            collective_id=0, has_side_effects=True, vmem_limit_bytes=32 << 20
+        ),
+    )(tiles, own_filter)
+
+
+def reduce_kernel(n_src, n_rcv, g_ref, o_rcv, o_src, parts, mine, s_p, r_p, s_a, r_a, s_b, r_b):
+    S, R = lax.axis_index("src"), lax.axis_index("rcv")
+    bar = pltpu.get_barrier_semaphore()
+    for k in range(1, n_src):
+        pl.semaphore_signal(bar, inc=1, device_id=(lax.rem(S + k, n_src), R), device_id_type=MESH)
+    for k in range(1, n_rcv):
+        pl.semaphore_signal(bar, inc=1, device_id=(S, lax.rem(R + k, n_rcv)), device_id_type=MESH)
+    pl.semaphore_wait(bar, n_src + n_rcv - 2)
+
+    def send_part(k, c):
+        d = lax.rem(S + k, n_src)
+        pltpu.make_async_remote_copy(
+            g_ref.at[d], parts.at[S], s_p, r_p, device_id=(d, R), device_id_type=MESH
+        ).start()
+        return c
+
+    lax.fori_loop(1, n_src, send_part, 0)
+    parts[S] = g_ref[S]
+    wait_bytes(parts.at[pl.ds(0, n_src - 1)], r_p)
+    total = jnp.sum(parts[...], axis=0)
+    mine[0] = total[:4]
+    mine[1] = total[4:]
+    o_rcv[S] = total[:4]
+    o_src[R] = total[4:]
+
+    def send_rcv(k, c):
+        pltpu.make_async_remote_copy(
+            mine.at[1], o_src.at[R], s_b, r_b, device_id=(S, lax.rem(R + k, n_rcv)), device_id_type=MESH
+        ).start()
+        return c
+
+    lax.fori_loop(1, n_rcv, send_rcv, 0)
+
+    def send_src(k, c):
+        pltpu.make_async_remote_copy(
+            mine.at[0], o_rcv.at[S], s_a, r_a, device_id=(lax.rem(S + k, n_src), R), device_id_type=MESH
+        ).start()
+        return c
+
+    lax.fori_loop(1, n_src, send_src, 0)
+    wait_bytes(o_rcv.at[pl.ds(0, n_src - 1)], r_a)
+    wait_bytes(o_src.at[pl.ds(0, n_rcv - 1)], r_b)
+    wait_bytes(parts.at[pl.ds(0, n_src - 1)], s_p)
+    wait_bytes(o_rcv.at[pl.ds(0, n_src - 1)], s_a)
+    wait_bytes(o_src.at[pl.ds(0, n_rcv - 1)], s_b)
+
+
+def reduce_both(parts, n_rcv):
+    n_src = parts.shape[0]
+    vm = pl.BlockSpec(memory_space=pltpu.VMEM)
+    D = pltpu.SemaphoreType.DMA
+    return pl.pallas_call(
+        functools.partial(reduce_kernel, n_src, n_rcv),
+        out_shape=(
+            jax.ShapeDtypeStruct((n_src, 4, 128), jnp.float32),
+            jax.ShapeDtypeStruct((n_rcv, 4, 128), jnp.float32),
+        ),
+        in_specs=[vm],
+        out_specs=(vm, vm),
+        scratch_shapes=[
+            pltpu.VMEM((n_src, 8, 128), jnp.float32),
+            pltpu.VMEM((2, 4, 128), jnp.float32),
+            D, D, D, D, D, D,
+        ],
+        compiler_params=pltpu.CompilerParams(collective_id=1, has_side_effects=True),
+    )(parts)
 
 
 def toeplitz_tables(tap_rows, trace_len):
@@ -69,7 +245,11 @@
     src_count = lax.axis_size("src")
     rcv_count = lax.axis_size("rcv")
     fine_size = src_rows // rcv_count
-    filter_table = lax.all_gather(filters, ("src", "rcv"), axis=0, tiled=True)
+    tiles = traces.reshape(rcv_count, 2, src_count, 2, 4, 128).transpose(2, 0, 3, 1, 4, 5)
+    tiles = tiles.reshape(src_count, rcv_count, 16, 128)
+    own_filter = jnp.pad(filters.astype(jnp.float32).reshape(4, 128), ((0, 4), (0, 0)))
+    moved, table = exchange(tiles, own_filter)
+    filter_table = table.reshape(src_count * rcv_count, 8, 128)[:, :4].reshape(-1, tap_count)
     local_rows = jnp.arange(src_rows, dtype=jnp.int32)
     local_cols = jnp.arange(rcv_cols, dtype=jnp.int32)
     row_slots = lax.axis_index("src") * src_rows + local_rows
@@ -78,15 +258,8 @@
     ) * fine_size + local_cols % fine_size
     row_taps = filter_table[station_of_slot[row_slots]]
     col_taps = filter_table[station_of_slot[col_slots]]
-    blocks = traces.reshape(rcv_count, fine_size, src_count, fine_size, trace_len)
-    moved = lax.all_to_all(
-        lax.all_to_all(blocks, "src", split_axis=2, concat_axis=2, tiled=True),
-        "rcv",
-        split_axis=0,
-        concat_axis=0,
-        tiled=True,
-    )
-    mirrored = moved.transpose(0, 3, 2, 1, 4).reshape(src_rows, rcv_cols, trace_len)
+    mirrored = moved.reshape(src_count, rcv_count, 2, 2, 4, 128).transpose(1, 2, 0, 3, 4, 5)
+    mirrored = mirrored.reshape(src_rows, rcv_cols, trace_len)
     by_column = jnp.transpose(traces, (1, 0, 2))
     column_filtered = convolve(by_column, col_taps)
     row_filtered = convolve(mirrored, row_taps)
@@ -101,7 +274,9 @@
     scale = 1.0 / math.sqrt(src_rows * src_count * trace_len)
     receiver_terms = correlate(jnp.transpose(residual, (1, 0, 2)), by_column, tap_count) * scale
     source_terms = correlate(residual, mirrored, tap_count) * -scale
-    grad_receiver = lax.psum(receiver_terms.astype(jnp.bfloat16), "src").astype(jnp.float32)
+    grad_receiver = receiver_terms.reshape(src_count, 4, 128)
+    sums_rcv, _ = reduce_both(jnp.concatenate([grad_receiver, grad_receiver], axis=1), rcv_count)
+    grad_receiver = sums_rcv.reshape(rcv_cols, tap_count)
     grad_source = lax.psum(source_terms.astype(jnp.bfloat16), "rcv").astype(jnp.float32)
     return (residual, grad_receiver, grad_source)
 

time: 1370 us -> 610 us (0.45)
  blocking collectives: 870 us -> 64.6 us
  Pallas kernels: 0 us -> 76.9 us
  starting transfers between devices: 14.5 us -> 0 us
    all_gather x1 -> x0, blocking collectives: 607 us -> none  [shards(): filter_table = lax.all_gather(filters, ('src', 'rcv'), axis=0, tiled=True)]
    psum x1 -> x0, blocking collectives: 194 us -> none  [shards(): lax.psum(receiver_terms.astype(jnp.bfloat16), 'src').astype(jnp.float32)]
    pallas_call x0 -> x2, Pallas kernels: none -> 76.9 us  [the longest x1 45.2 us: exchange(): pl.pallas_call(functools.partial(exchange_kernel, n_src, n_rcv), out_shap...]
    all_to_all x2 -> x0, starting transfers between devices: 14.5 us -> none  [the longest x1 7.34 us: shards(): lax.all_to_all(blocks, 'src', split_axis=2, concat_axis=2, tiled=True)]
  transfers between devices with their start and end apart: 2 -> 0, of which waited for: 0 -> 0; matrix products, arithmetic and copies ran while one was open for 11% -> 0% of each run, Pallas kernels for 0% -> 0%
where the time goes in v1:
time: 610 us; the launch traced here: 601 us
  local copies, waits for them, and re-layouts  385 us (63%)
  Pallas kernels  76.9 us (13%)
  blocking collectives  64.6 us (11%)
  matrix products  51.4 us (8%)
  other arithmetic  18.4 us (3%)
    reshape x16, local copies, waits for them, and re-layouts, toeplitz_tables(): return tiled.reshape(group_count, trace_len, period - 1)[:, :, :trace_len]  140 us
    while x112, local copies, waits for them, and re-layouts  121 us
    reshape x64, local copies, waits for them, and re-layouts, lag_group(): flattened.reshape(station_group, block_len, block_len + tap_count + 1)  65 us
    psum x1, blocking collectives, shards(): lax.psum(source_terms.astype(jnp.bfloat16), 'rcv').astype(jnp.float32)  64.6 us
    pallas_call x1, Pallas kernels, exchange(): pl.pallas_call(functools.partial(exchange_kernel, n_src, n_rcv), out_shap...  45.2 us
    dot_general x16, matrix products, filter_group(): jnp.einsum('gpu,gut->gpt', trace_block, tables, preferred_element_type=jn...  32.4 us
    pallas_call x1, Pallas kernels, reduce_both(): pl.pallas_call(functools.partial(reduce_kernel, n_src, n_rcv), out_shape=...  31.6 us
    dot_general x64, matrix products, lag_group(): jnp.einsum('gpa,gpj->gaj', residual_block[:, :, begin_at:begin_at + block...  19 us

profile of v1, /device:TPU:1, one launch (start us, length us, event | category | flops | bytes accessed | tf_op | source)
XLA Modules:
  0.0 601.0 jit_solution(5483980005561843964)
XLA Ops:
  2.5 45.2 %shard_map.67 = (bf16[16,16,16,128]{3,2,1,0:T(8,128)(2,1)S(1)}, bf16[16,128,128]{2,1,0:T(8,128)(2,1)S(1)}) custom-call(bf16[16,16,16,128]{3,2,1,0:T(8,128)(2,1)S(1)} %bitcast.152, f32[8,128]{1,0:T(8,128)S(1)} %pad_convert_fusion.f_ref), custom_call_target="tpu_custom_call" | custom-call | tf_op jit(solution)/shard_map/pallas_call | solution.py:100
  52.4 139.9 %while.45 = (s32[]{:T(128)}, bf16[8,4,32,512]{3,2,1,0:T(8,128)(2,1)}, bf16[8,4,32,512]{3,2,1,0:T(8,128)(2,1)}, bf16[8,4,256]{2,1,0:T(4,128)(2,1)S(1)}, s32[]{:T(128)}, /*index=5*/bf16[]{:T(256)}) while((s32[]{:T(128)}, bf16[8,4,32,512]{3,2,1,0:T(8,128)(2,1)}, bf16[8,4,32,512]{3,2,1,0:T(8,128)(2,1)}, bf16[8,4,256]{2,1,0:T(4,128)(2,1)S(1)}, ...), condition=%wide.region_3.4_spmd, body=%wide.region_2.3_spmd.sunk | while | flops 67174400 | bytes 30665804 | solution.py:210
  56.2 2.9 reshape.346
  59.1 8.8 %reshape.347 = bf16[4,512,767]{2,1,0:T(8,128)(2,1)S(1)} reshape(bf16[1570816]{0:T(1024)(128)(2,1)} %reshape.346) | data formatting | bytes 6283264 | tf_op jit(solution)/shard_map/while/body/eval_jaxpr/reshape | solution.py:194
  76.6 8.8 %reshape.347 = bf16[4,512,767]{2,1,0:T(8,128)(2,1)S(1)} reshape(bf16[1570816]{0:T(1024)(128)(2,1)} %reshape.346) | data formatting | bytes 6283264 | tf_op jit(solution)/shard_map/while/body/eval_jaxpr/reshape | solution.py:194
  94.1 8.8 %reshape.347 = bf16[4,512,767]{2,1,0:T(8,128)(2,1)S(1)} reshape(bf16[1570816]{0:T(1024)(128)(2,1)} %reshape.346) | data formatting | bytes 6283264 | tf_op jit(solution)/shard_map/while/body/eval_jaxpr/reshape | solution.py:194
  111.5 8.8 %reshape.347 = bf16[4,512,767]{2,1,0:T(8,128)(2,1)S(1)} reshape(bf16[1570816]{0:T(1024)(128)(2,1)} %reshape.346) | data formatting | bytes 6283264 | tf_op jit(solution)/shard_map/while/body/eval_jaxpr/reshape | solution.py:194
  129.0 8.8 %reshape.347 = bf16[4,512,767]{2,1,0:T(8,128)(2,1)S(1)} reshape(bf16[1570816]{0:T(1024)(128)(2,1)} %reshape.346) | data formatting | bytes 6283264 | tf_op jit(solution)/shard_map/while/body/eval_jaxpr/reshape | solution.py:194
  146.5 8.8 %reshape.347 = bf16[4,512,767]{2,1,0:T(8,128)(2,1)S(1)} reshape(bf16[1570816]{0:T(1024)(128)(2,1)} %reshape.346) | data formatting | bytes 6283264 | tf_op jit(solution)/shard_map/while/body/eval_jaxpr/reshape | solution.py:194
  164.0 8.8 %reshape.347 = bf16[4,512,767]{2,1,0:T(8,128)(2,1)S(1)} reshape(bf16[1570816]{0:T(1024)(128)(2,1)} %reshape.346) | data formatting | bytes 6283264 | tf_op jit(solution)/shard_map/while/body/eval_jaxpr/reshape | solution.py:194
  181.5 8.8 %reshape.347 = bf16[4,512,767]{2,1,0:T(8,128)(2,1)S(1)} reshape(bf16[1570816]{0:T(1024)(128)(2,1)} %reshape.346) | data formatting | bytes 6283264 | tf_op jit(solution)/shard_map/while/body/eval_jaxpr/reshape | solution.py:194
  197.6 140.6 %while.44 = (s32[]{:T(128)}, bf16[8,4,32,512]{3,2,1,0:T(8,128)(2,1)}, bf16[8,4,32,512]{3,2,1,0:T(8,128)(2,1)}, bf16[8,4,256]{2,1,0:T(4,128)(2,1)S(1)}, s32[]{:T(128)}, /*index=5*/bf16[]{:T(256)}) while((s32[]{:T(128)}, bf16[8,4,32,512]{3,2,1,0:T(8,128)(2,1)}, bf16[8,4,32,512]{3,2,1,0:T(8,128)(2,1)}, bf16[8,4,256]{2,1,0:T(4,128)(2,1)S(1)}, ...), condition=%wide.region_1.2_spmd, body=%wide.region_0.1_spmd.sunk | while | flops 67174400 | bytes 30665804 | solution.py:210
  201.9 2.9 reshape.344
  204.8 8.8 %reshape.345 = bf16[4,512,767]{2,1,0:T(8,128)(2,1)S(1)} reshape(bf16[1570816]{0:T(1024)(128)(2,1)} %reshape.344) | data formatting | bytes 6283264 | tf_op jit(solution)/shard_map/while/body/eval_jaxpr/reshape | solution.py:194
  219.4 2.9 reshape.344
  222.3 8.8 %reshape.345 = bf16[4,512,767]{2,1,0:T(8,128)(2,1)S(1)} reshape(bf16[1570816]{0:T(1024)(128)(2,1)} %reshape.344) | data formatting | bytes 6283264 | tf_op jit(solution)/shard_map/while/body/eval_jaxpr/reshape | solution.py:194
  236.9 2.9 reshape.344
  239.8 8.8 %reshape.345 = bf16[4,512,767]{2,1,0:T(8,128)(2,1)S(1)} reshape(bf16[1570816]{0:T(1024)(128)(2,1)} %reshape.344) | data formatting | bytes 6283264 | tf_op jit(solution)/shard_map/while/body/eval_jaxpr/reshape | solution.py:194
  254.4 2.9 reshape.344
  257.3 8.8 %reshape.345 = bf16[4,512,767]{2,1,0:T(8,128)(2,1)S(1)} reshape(bf16[1570816]{0:T(1024)(128)(2,1)} %reshape.344) | data formatting | bytes 6283264 | tf_op jit(solution)/shard_map/while/body/eval_jaxpr/reshape | solution.py:194
  271.9 2.9 reshape.344
  274.8 8.8 %reshape.345 = bf16[4,512,767]{2,1,0:T(8,128)(2,1)S(1)} reshape(bf16[1570816]{0:T(1024)(128)(2,1)} %reshape.344) | data formatting | bytes 6283264 | tf_op jit(solution)/shard_map/while/body/eval_jaxpr/reshape | solution.py:194
  289.4 2.9 reshape.344
  292.3 8.8 %reshape.345 = bf16[4,512,767]{2,1,0:T(8,128)(2,1)S(1)} reshape(bf16[1570816]{0:T(1024)(128)(2,1)} %reshape.344) | data formatting | bytes 6283264 | tf_op jit(solution)/shard_map/while/body/eval_jaxpr/reshape | solution.py:194
  307.0 2.9 reshape.344
  309.8 8.8 %reshape.345 = bf16[4,512,767]{2,1,0:T(8,128)(2,1)S(1)} reshape(bf16[1570816]{0:T(1024)(128)(2,1)} %reshape.344) | data formatting | bytes 6283264 | tf_op jit(solution)/shard_map/while/body/eval_jaxpr/reshape | solution.py:194
  324.5 2.9 reshape.344
  327.3 8.8 %reshape.345 = bf16[4,512,767]{2,1,0:T(8,128)(2,1)S(1)} reshape(bf16[1570816]{0:T(1024)(128)(2,1)} %reshape.344) | data formatting | bytes 6283264 | tf_op jit(solution)/shard_map/while/body/eval_jaxpr/reshape | solution.py:194
  341.2 80.1 %while.47 = (s32[]{:T(128)}, f32[8,4,256]{2,1,0:T(4,128)S(1)}, bf16[8,4,32,512]{3,2,1,0:T(8,128)(2,1)S(1)}, bf16[8,4,32,512]{3,2,1,0:T(8,128)(2,1)}, s32[]{:T(128)}, /*index=5*/f32[]{:T(128)}) while((s32[]{:T(128)}, f32[8,4,256]{2,1,0:T(4,128)S(1)}, bf16[8,4,32,512]{3,2,1,0:T(8,128)(2,1)S(1)}, bf16[8,4,32,512]{3,2,1,0:T(8,128)(2,1)}, ...), condition=%wide.region_15.16_spmd, body=%wide.region_10.15_spmd.sunk | while | flops 50854912 | bytes 25309276 | solution.py:239
  421.4 64.6 %psum.7 = bf16[32,256]{1,0:T(8,128)(2,1)S(1)} all-reduce(bf16[32,256]{1,0:T(8,128)(2,1)S(1)} %convert_element_type.54), channel_id=1, replica_groups=mesh['src'=16,'rcv'=16] {'rcv'}, use_global_device_ids=true, to_apply=%region_16.17 | all-reduce | flops 8192 | bytes 32768 | tf_op jit(solution)/shard_map/psum | solution.py:280
  487.2 79.9 %while.46 = (s32[]{:T(128)}, f32[8,4,256]{2,1,0:T(4,128)S(1)}, bf16[8,4,32,512]{3,2,1,0:T(8,128)(2,1)S(1)}, bf16[8,4,32,512]{3,2,1,0:T(8,128)(2,1)}, s32[]{:T(128)}, /*index=5*/f32[]{:T(128)}) while((s32[]{:T(128)}, f32[8,4,256]{2,1,0:T(4,128)S(1)}, bf16[8,4,32,512]{3,2,1,0:T(8,128)(2,1)S(1)}, bf16[8,4,32,512]{3,2,1,0:T(8,128)(2,1)}, ...), condition=%wide.region_9.10_spmd, body=%wide.region_4.9_spmd.sunk | while | flops 50854912 | bytes 25309276 | solution.py:239
  567.8 31.6 %shard_map.68 = (f32[16,4,128]{2,1,0:T(4,128)}, f32[16,4,128]{2,1,0:T(4,128)}) custom-call(f32[16,8,128]{2,1,0:T(8,128)} %pad_maximum_fusion.g_ref), custom_call_target="tpu_custom_call" | custom-call | tf_op jit(solution)/shard_map/pallas_call | solution.py:170
  (537 shorter events, 288.9 us)
Async XLA Ops:
  0.6 47.4 %copy-start = (s32[512]{0:T(512)S(1)}, s32[512]{0:T(512)}, u32[]{:S(2)}) copy-start(s32[512]{0:T(512)} %param.15) | copy-start | bytes 6148
  0.6 1.9 copy-start.5
  338.2 1.6 copy-start.4
  338.2 1.6 copy-start.3
  421.3 65.8 %copy-start.2 = (bf16[8,4,32,512]{3,2,1,0:T(8,128)(2,1)}, bf16[8,4,32,512]{3,2,1,0:T(8,128)(2,1)S(1)}, u32[]{:S(2)}) copy-start(bf16[8,4,32,512]{3,2,1,0:T(8,128)(2,1)S(1)} %get-tuple-element.387) | copy-start | bytes 3145732
  567.1 33.7 %copy-start.1 = (s32[512]{0:T(512)S(1)}, s32[512]{0:T(512)}, u32[]{:S(2)}) copy-start(s32[512]{0:T(512)} %param.15) | copy-start | bytes 6148

commit v2 on v0

v2 whole, which is shorter than its diff:
```python
import functools
import math

import jax
import jax.numpy as jnp
from jax import lax
from jax.experimental import pallas as pl
from jax.experimental.pallas import tpu as pltpu
from jax.sharding import PartitionSpec as P

MESH = pl.DeviceIdType.MESH
F32 = jnp.float32
BF16 = jnp.bfloat16
NB = 4
L = 128


def digits_of(n_src, n_rcv):
    if (n_src, n_rcv) == (16, 16):
        return (2, 4, 2), (4, 4)
    return (1, n_src // 2, 2), (n_rcv // 2, 2)


def line_peers(S, R, n_src, n_rcv):
    (nl, ny, nc), (nx, nh) = digits_of(n_src, n_rcv)
    l, y, c = S // (ny * nc), lax.rem(S // nc, ny), lax.rem(S, nc)
    x, h = R // nh, lax.rem(R, nh)

    def at(dl, dy, dc, dx, dh):
        s = (lax.rem(l + dl, nl) * ny + lax.rem(y + dy, ny)) * nc + lax.rem(c + dc, nc)
        return s, lax.rem(x + dx, nx) * nh + lax.rem(h + dh, nh)

    z = [at(a, 0, 0, 0, b) for a in range(nl) for b in range(nh) if a or b]
    xs = [at(0, 0, 0, a, 0) for a in range(1, nx)]
    ys = [at(0, a, 0, 0, 0) for a in range(1, ny)]
    cs = [at(0, 0, a, 0, 0) for a in range(1, nc)]
    return z, xs, ys, cs


def wait_bytes(ref, sem):
    pltpu.make_async_copy(ref, ref, sem).wait()


def iota(shape, axis):
    return lax.broadcasted_iota(jnp.int32, shape, axis)


def swap_middle(v, rows):
    place = lax.rem(iota((rows, L), 0), 16) // 4
    down = pltpu.roll(v, 4, 0)
    up = pltpu.roll(v, rows - 4, 0)
    return jnp.where(place == 1, up, jnp.where(place == 2, down, v))


def kernel(
    n_src, n_rcv, scale,
    traces, mask, filters, slots,
    residual, grad_rcv, grad_src,
    xin, xt, x3, x3t, floc, send, recv, res,
    m128, mt, fm, f_row, table, tabf, ctaps, g128, gsnd, hrec, pown, prec, toep,
    gmsg, parts, mine,
    stage_sems, s_in, s_x, r_x, s_f, r_f, s_g, r_g, s_h, r_h, s_p, r_p, s_a, r_a, s_b, r_b,
):
    S, R = lax.axis_index("src"), lax.axis_index("rcv")
    rows_p, cols_q = 2 * n_rcv, 2 * n_src
    rows = n_rcv * 16

    z, xs, ys, cs = line_peers(S, R, n_src, n_rcv)
    bar = pltpu.get_barrier_semaphore()
    near = z + xs + ys + cs
    for d in near:
        pl.semaphore_signal(bar, inc=1, device_id=d, device_id_type=MESH)
    load = pltpu.make_async_copy(traces, xin, s_in)
    load.start()

    m128[...] = jnp.zeros((L, L), F32)
    m128[0:rows_p, 0:cols_q] = mask[...].astype(F32)
    mt[...] = jnp.transpose(m128[...])
    f = filters[...].astype(F32)
    fm[...] = jnp.zeros(fm.shape, F32)
    for r in range(n_rcv):
        fm[r, 0:2, :] = f[:, :L]
        fm[r, 2:4, :] = f[:, L:]
        fm[r, 4:6, :] = m128[2 * r : 2 * r + 2, :]

    pl.semaphore_wait(bar, len(near))
    for i, group in enumerate((xs, ys, cs)):
        for d in group:
            pl.semaphore_signal(stage_sems.at[i], inc=1, device_id=d, device_id_type=MESH)
        pl.semaphore_wait(stage_sems.at[i], len(group))

    own8 = pl.ds(pl.multiple_of(R * 8, 8), 8)

    def send_filter(j, c):
        d = lax.rem(R + j, n_rcv)
        pltpu.make_async_remote_copy(
            fm.at[d], f_row.at[own8], s_f, r_f, device_id=(S, d), device_id_type=MESH
        ).start()
        return c

    lax.fori_loop(1, n_rcv, send_filter, 0)
    f_row[own8, :] = fm[R]

    load.wait()

    def spread(p, c):
        for b in range(NB):
            xt[p, pl.ds(b, cols_q, stride=NB), :] = xin[p, :, b * L : (b + 1) * L].astype(F32)
        return c

    lax.fori_loop(0, rows_p, spread, 0)
    row = iota((rows, L), 0)
    lane = iota((rows, L), 1)
    block = lax.rem(row, NB)
    q2 = lax.rem(row // NB, 2)
    p2 = lax.rem(row // (2 * NB), 2)
    tile = row // 16
    pown[...] = jnp.where(lane == 2 * tile + p2, 1.0, 0.0)
    prec[...] = jnp.where(lane == 64 + q2 * n_rcv + tile, 1.0, 0.0)
    flip = jnp.where(iota((L, L), 0) + iota((L, L), 1) == L - 1, 1.0, 0.0).astype(BF16)

    def delays(s, c):
        x = xt[:, pl.ds(pl.multiple_of(s * 8, 8), 8), :].reshape(rows, L)
        for d in range(3):
            v = x if d == 0 else jnp.where(block >= d, pltpu.roll(x, d, 0), 0.0)
            v = v.astype(BF16)
            at = (2 - d) * L
            x3[s, :, at : at + L] = v
            x3t[s, at : at + L, :] = lax.dot_general(
                flip, v, (((1,), (1,)), ((), ())), preferred_element_type=F32
            ).astype(BF16)
        return c

    lax.fori_loop(0, n_src, delays, 0)

    wait_bytes(f_row.at[pl.ds(0, (n_rcv - 1) * 8)], r_f)
    for i in range(4):
        table[S, i * n_rcv : (i + 1) * n_rcv, :] = f_row[pl.ds(i, n_rcv, stride=8), :].astype(BF16)
    g128[...] = jnp.zeros((L, L), F32)
    for i in range(2):
        g128[64 + i * n_rcv : 64 + (i + 1) * n_rcv, :] = f_row[pl.ds(4 + i, n_rcv, stride=8), :]
    gt = jnp.transpose(g128[...])
    gsnd[...] = jnp.zeros(gsnd.shape, F32)
    for s in range(n_src):
        gsnd[s, 0:2, :] = gt[2 * s : 2 * s + 2, :]

    def send_rows(k, c):
        d = lax.rem(S + k, n_src)
        pltpu.make_async_remote_copy(
            table.at[S], table.at[S], s_g, r_g, device_id=(d, R), device_id_type=MESH
        ).start()
        pltpu.make_async_remote_copy(
            gsnd.at[d], hrec.at[S], s_h, r_h, device_id=(d, R), device_id_type=MESH
        ).start()
        return c

    lax.fori_loop(1, n_src, send_rows, 0)
    hrec[S] = gsnd[S]
    wait_bytes(table.at[pl.ds(0, n_src - 1)], r_g)
    tabf[...] = table[...].astype(F32).reshape(tabf.shape)

    def pick(w, c):
        slot = ((w // 2) * n_rcv + R) * 2 + lax.rem(w, 2)
        st = slots[slot]
        at = (st // (2 * n_rcv)) * (4 * n_rcv) + lax.rem(st, 2) * n_rcv + lax.rem(st // 2, n_rcv)
        ctaps[pl.ds(w, 1), :] = tabf[pl.ds(at, 1), :]
        ctaps[pl.ds(cols_q + w, 1), :] = tabf[pl.ds(at + 2 * n_rcv, 1), :]
        return c

    lax.fori_loop(0, cols_q, pick, 0)

    later = iota((L, L), 1) >= iota((L, L), 0)

    def filter_pair(k, first):
        s = lax.rem(S + k, n_src)
        for i in range(2):
            q = 2 * s + i
            c0 = jnp.broadcast_to(ctaps[pl.ds(q, 1), :], (L, L))
            c1 = jnp.broadcast_to(ctaps[pl.ds(cols_q + q, 1), :], (L, L))
            c0 = pltpu.roll(c0, 0, 1, stride=1, stride_axis=0)
            c1 = pltpu.roll(c1, 0, 1, stride=1, stride_axis=0)
            at = slice(i * L, (i + 1) * L)
            toep[0:L, at] = jnp.where(later, 0.0, c1).astype(BF16)
            toep[L : 2 * L, at] = jnp.where(later, c1, c0).astype(BF16)
            toep[2 * L : 3 * L, at] = jnp.where(later, c0, 0.0).astype(BF16)
        y = jnp.dot(x3[s], toep[...], preferred_element_type=F32)
        y = jnp.where(q2 == 1, y[:, L:], y[:, :L]).astype(BF16)
        floc[s] = y
        send[s] = swap_middle(y.astype(F32), rows).astype(BF16).reshape(n_rcv, 16, L)
        for j in range(1 if first else 0, n_rcv):
            d = lax.rem(R + j, n_rcv)
            pltpu.make_async_remote_copy(
                send.at[s, d], recv.at[S, R], s_x, r_x.at[k], device_id=(s, d), device_id_type=MESH
            ).start()

    filter_pair(0, True)
    recv[S, R] = send[S, R]

    def filter_step(k, c):
        filter_pair(k, False)
        return c

    lax.fori_loop(1, n_src, filter_step, 0)
    wait_bytes(hrec.at[pl.ds(0, n_src - 1)], r_h)

    reach = iota((L, L), 1) + iota((L, L), 0) >= L - 1
    spread_ones = jnp.where((iota((L, 2 * L), 0) < 64) == (iota((L, 2 * L), 1) < L), 1.0, 0.0).astype(BF16)

    def lag_pair(k, first):
        s = lax.rem(S + n_src - k, n_src)
        wait_bytes(recv.at[0, pl.ds(0, n_rcv - (1 if first else 0))], r_x.at[k])
        diff = floc[s].astype(F32) - recv[s].reshape(rows, L).astype(F32)
        own = jnp.where(q2 == 0, mt[pl.ds(2 * s, 1), :], mt[pl.ds(2 * s + 1, 1), :])
        other = jnp.where(p2 == 0, hrec[s, 0:1, :], hrec[s, 1:2, :])
        live = pown[...] * own + prec[...] * other
        live = jnp.dot(live.astype(BF16), spread_ones, preferred_element_type=F32)
        found = []
        for t in range(2):
            r = live[:, t * L : (t + 1) * L] * diff
            if t == 0:
                res[:, pl.ds(pl.multiple_of(s * 8, 8), 8), :] = r.reshape(rows_p, 8, L)
            both = jnp.concatenate([jnp.where(q2 == 0, r, 0.0), jnp.where(q2 == 1, r, 0.0)], axis=1)
            m = jnp.dot(x3t[s], both.astype(BF16), preferred_element_type=F32)
            for i in range(2):
                mi = m[:, i * L : (i + 1) * L]
                m2, m1, m0 = mi[0:L], mi[L : 2 * L], mi[2 * L : 3 * L]
                for a, b in ((m0, m1), (m1, m2)):
                    skew = pltpu.roll(jnp.where(reach, a, b), 1, 1, stride=1, stride_axis=0)
                    found.append(jnp.sum(skew, axis=0, keepdims=True))
        msg = jnp.concatenate(found, axis=0)
        if first:
            parts[S] = msg
        else:
            gmsg[s] = msg
            pltpu.make_async_remote_copy(
                gmsg.at[s], parts.at[S], s_p, r_p, device_id=(s, R), device_id_type=MESH
            ).start()

    lag_pair(0, True)

    def lag_step(k, c):
        lag_pair(k, False)
        return c

    lax.fori_loop(1, n_src, lag_step, 0)

    def gather(p, c):
        for b in range(NB):
            residual[p, :, b * L : (b + 1) * L] = res[p, pl.ds(b, cols_q, stride=NB), :].astype(BF16)
        return c

    lax.fori_loop(0, rows_p, gather, 0)

    wait_bytes(parts.at[pl.ds(0, n_src - 1)], r_p)
    total = jnp.sum(parts[...], axis=0) * scale
    mine[0] = total[:4]
    mine[1] = total[4:]
    grad_rcv[S] = total[:4]
    grad_src[R] = total[4:]

    def send_rcv(k, c):
        pltpu.make_async_remote_copy(
            mine.at[1], grad_src.at[R], s_b, r_b, device_id=(S, lax.rem(R + k, n_rcv)), device_id_type=MESH
        ).start()
        return c

    lax.fori_loop(1, n_rcv, send_rcv, 0)

    def send_src(k, c):
        pltpu.make_async_remote_copy(
            mine.at[0], grad_rcv.at[S], s_a, r_a, device_id=(lax.rem(S + k, n_src), R), device_id_type=MESH
        ).start()
        return c

    lax.fori_loop(1, n_src, send_src, 0)
    wait_bytes(f_row.at[pl.ds(0, (n_rcv - 1) * 8)], s_f)
    wait_bytes(table.at[pl.ds(0, n_src - 1)], s_g)
    wait_bytes(hrec.at[pl.ds(0, n_src - 1)], s_h)
    wait_bytes(parts.at[pl.ds(0, n_src - 1)], s_p)
    for k in range(n_src):
        wait_bytes(recv.at[0, pl.ds(0, n_rcv - (k == 0))], s_x)
    wait_bytes(grad_rcv.at[pl.ds(0, n_src - 1)], r_a)
    wait_bytes(grad_src.at[pl.ds(0, n_rcv - 1)], r_b)
    wait_bytes(grad_rcv.at[pl.ds(0, n_src - 1)], s_a)
    wait_bytes(grad_src.at[pl.ds(0, n_rcv - 1)], s_b)


def shards(traces, dead_mask, filters, station_of_slot):
    rows_p, cols_q, trace_len = traces.shape
    tap_count = filters.shape[1]
    n_src, n_rcv = lax.axis_size("src"), lax.axis_size("rcv")
    rows = n_rcv * 16
    scale = 1.0 / math.sqrt(rows_p * n_src * trace_len)
    vm = pl.BlockSpec(memory_space=pltpu.VMEM)
    V = pltpu.VMEM
    D = pltpu.SemaphoreType.DMA
    residual, grad_rcv, grad_src = pl.pallas_call(
        functools.partial(kernel, n_src, n_rcv, scale),
        out_shape=(
            jax.ShapeDtypeStruct(traces.shape, BF16),
            jax.ShapeDtypeStruct((n_src, 4, L), F32),
            jax.ShapeDtypeStruct((n_rcv, 4, L), F32),
        ),
        in_specs=[pl.BlockSpec(memory_space=pl.ANY), vm, vm, pl.BlockSpec(memory_space=pltpu.SMEM)],
        out_specs=(vm, vm, vm),
        scratch_shapes=[
            V(traces.shape, BF16),
            V((rows_p, NB * cols_q, L), F32),
            V((n_src, rows, 3 * L), BF16),
            V((n_src, 3 * L, rows), BF16),
            V((n_src, rows, L), BF16),
            V((n_src, n_rcv, 16, L), BF16),
            V((n_src, n_rcv, 16, L), BF16),
            V((rows_p, NB * cols_q, L), F32),
            V((L, L), F32),
            V((L, L), F32),
            V((n_rcv, 8, L), F32),
            V((n_rcv * 8, L), F32),
            V((n_src, 4 * n_rcv, L), BF16),
            V((n_src * 4 * n_rcv, L), F32),
            V((2 * cols_q, L), F32),
            V((L, L), F32),
            V((n_src, 8, L), F32),
            V((n_src, 8, L), F32),
            V((rows, L), F32),
            V((rows, L), F32),
            V((3 * L, 2 * L), BF16),
            V((n_src, 8, L), F32),
            V((n_src, 8, L), F32),
            V((2, 4, L), F32),
            pltpu.SemaphoreType.REGULAR((3,)),
            D, D, D((n_src,)), D, D, D, D, D, D, D, D, D, D, D, D,
        ],
        compiler_params=pltpu.CompilerParams(
            collective_id=0, has_side_effects=True, vmem_limit_bytes=48 << 20
        ),
    )(traces, dead_mask, filters, station_of_slot)
    return residual, grad_rcv.reshape(cols_q, tap_count), grad_src.reshape(rows_p, tap_count)


def solution(mesh):
    placed = (P("src", "rcv", None), P("src", "rcv"), P(("src", "rcv"), None), P())
    return jax.shard_map(
        shards,
        mesh=mesh,
        in_specs=placed,
        out_specs=(P("src", "rcv", None), P("rcv", None), P("src", None)),
        check_vma=False,
    )
```

time: 1370 us -> 70.2 us (0.05); the launches traced: 1350 us -> 69.9 us
  blocking collectives: 870 us -> 0 us
  local copies, waits for them, and re-layouts: 388 us -> 5.53 us
  Pallas kernels: 0 us -> 63.8 us
  matrix products: 51.5 us -> 0 us
  other arithmetic: 21.3 us -> 0 us
  starting transfers between devices: 14.5 us -> 0 us
    all_gather x1 -> x0, blocking collectives: 607 us -> none  [shards(): filter_table = lax.all_gather(filters, ('src', 'rcv'), axis=0, tiled=True)]
    psum x2 -> x0, blocking collectives: 263 us -> none  [the longest x1 194 us: shards(): lax.psum(receiver_terms.astype(jnp.bfloat16), 'src').astype(jnp.float32)]
    reshape x84 -> x2, local copies, waits for them, and re-layouts: 209 us -> 1.27 us  [the longest x1 0.63 us: shards(): grad_rcv.reshape(cols_q, tap_count)]
    while x113 -> x0, local copies, waits for them, and re-layouts: 121 us -> none
    pallas_call x0 -> x1, Pallas kernels: none -> 63.8 us  [shards(): pl.pallas_call(functools.partial(kernel, n_src, n_rcv, scale), out_shape=...]
    dot_general x80 -> x0, matrix products: 51.5 us -> none  [the longest x16 32.4 us: filter_group(): jnp.einsum('gpu,gut->gpt', trace_block, tables, preferred_element_type=jn...]
    slice x16 -> x0, local copies, waits for them, and re-layouts: 18.4 us -> none  [toeplitz_tables(): tiled = jnp.tile(padded, (1, trace_len))[:, :trace_len * (period - 1)]]
    squeeze x32 -> x0, local copies, waits for them, and re-layouts: 14.9 us -> none  [convolve(): lax.map(filter_group, (grouped, grouped_taps))]
  transfers between devices with their start and end apart: 2 -> 0, of which waited for: 0 -> 0; matrix products, arithmetic and copies ran while one was open for 11% -> 0% of each run, Pallas kernels for 0% -> 0%
where the time goes in v2:
time: 70.2 us; the launch traced here: 69.9 us
  Pallas kernels  63.8 us (91%)
  local copies, waits for them, and re-layouts  5.53 us (8%)
    pallas_call x1, Pallas kernels, shards(): pl.pallas_call(functools.partial(kernel, n_src, n_rcv, scale), out_shape=...  63.8 us
    unnamed x9, local copies, waits for them, and re-layouts  4.26 us

profile of v2, /device:TPU:1, one launch (start us, length us, event | category | flops | bytes accessed | tf_op | source)
XLA Modules:
  0.0 69.9 jit_solution(9694329744232399832)
XLA Ops:
  0.6 0.0 copy-start
  0.6 1.2 %copy-done = bf16[32,32,512]{2,1,0:T(8,128)(2,1)S(1)} copy-done((bf16[32,32,512]{2,1,0:T(8,128)(2,1)S(1)}, bf16[32,32,512]{2,1,0:T(8,128)(2,1)}, u32[]{:S(2)}) %copy-start) | copy-done | bytes 1048600
  1.9 0.0 copy-start.1
  1.9 0.7 %copy-done.1 = s32[32,32]{1,0:T(8,128)S(1)} copy-done((s32[32,32]{1,0:T(8,128)S(1)}, s32[32,32]{1,0:T(8,128)}, u32[]{:S(2)}) %copy-start.1) | copy-done | bytes 4120
  2.6 0.0 copy-start.2
  2.6 0.7 copy-done.2
  3.3 0.0 copy-start.3
  3.3 0.7 copy-done.3
  3.9 63.8 %shard_map.67 = (bf16[32,32,512]{2,1,0:T(8,128)(2,1)S(1)}, f32[16,4,128]{2,1,0:T(4,128)S(1)}, f32[16,4,128]{2,1,0:T(4,128)S(1)}) custom-call(bf16[32,32,512]{2,1,0:T(8,128)(2,1)S(1)} %copy-done, s32[32,32]{1,0:T(8,128)S(1)} %copy-done.1, bf16[2,256]{1,0:T(2,128)(2,1)S(1)} %copy-done.3, s32[512]{0:T(512)S(1)} %copy-done.2), custom_call_target="tpu_custom_call" | custom-call | tf_op jit(solution)/shard_map/pallas_call | solution.py:297
  67.7 0.6 reshape.12
  68.3 0.6 reshape.13
  69.0 1.0 %copy.8 = bf16[32,32,512]{2,1,0:T(8,128)(2,1)} copy(bf16[32,32,512]{2,1,0:T(8,128)(2,1)S(1)} %get-tuple-element.12) | data formatting | bytes 2097152
Async XLA Ops:
  0.6 1.2 %copy-start = (bf16[32,32,512]{2,1,0:T(8,128)(2,1)S(1)}, bf16[32,32,512]{2,1,0:T(8,128)(2,1)}, u32[]{:S(2)}) copy-start(bf16[32,32,512]{2,1,0:T(8,128)(2,1)} %traces.1) | copy-start | bytes 3145732
  1.9 0.7 %copy-start.1 = (s32[32,32]{1,0:T(8,128)S(1)}, s32[32,32]{1,0:T(8,128)}, u32[]{:S(2)}) copy-start(s32[32,32]{1,0:T(8,128)} %mask.1) | copy-start | bytes 12292
  2.6 0.7 copy-start.2
  3.3 0.7 copy-start.3

commit v3 on v2

v3 whole, which is shorter than its diff:
```python
import functools
import math

import jax
import jax.numpy as jnp
from jax import lax
from jax.experimental import pallas as pl
from jax.experimental.pallas import tpu as pltpu
from jax.sharding import PartitionSpec as P

MESH = pl.DeviceIdType.MESH
F32 = jnp.float32
BF16 = jnp.bfloat16
NB = 4
L = 128
RAW = 4


def digits_of(n_src, n_rcv):
    if (n_src, n_rcv) == (16, 16):
        return (2, 4, 2), (4, 4)
    return (1, n_src // 2, 2), (n_rcv // 2, 2)


def rcv_offsets(nx, nh):
    def far(d):
        return 2 * min(d[1], nh - d[1]), min(d[0], nx - d[0])

    return sorted([(a, b) for a in range(nx) for b in range(nh)], key=far, reverse=True)


def raw_of(n_rcv):
    return n_rcv * RAW // 16


def wait_bytes(ref, sem):
    pltpu.make_async_copy(ref, ref, sem).wait()


def iota(shape, axis):
    return lax.broadcasted_iota(jnp.int32, shape, axis)


def swap_middle(a, b):
    low = iota(a.shape, 1) < 4
    ra, rb = pltpu.roll(a, 4, 1), pltpu.roll(b, 4, 1)
    w0, w1 = jnp.where(low, a, rb), jnp.where(low, ra, b)
    return jnp.concatenate([w0, w1], axis=1).astype(BF16)


def delayed(x):
    block = lax.rem(iota(x.shape, 1), NB)
    n = x.shape[0] * 8
    out = [x]
    for d in (1, 2):
        out.append(jnp.where(block >= d, pltpu.roll(x, d, 1), 0.0))
    return [v.reshape(n, L).astype(BF16) for v in out]


def toeplitz(c0, c1, later, out, at):
    c0 = pltpu.roll(jnp.broadcast_to(c0, (L, L)), 0, 1, stride=1, stride_axis=0)
    c1 = pltpu.roll(jnp.broadcast_to(c1, (L, L)), 0, 1, stride=1, stride_axis=0)
    out[0:L, at : at + L] = jnp.where(later, 0.0, c1).astype(BF16)
    out[L : 2 * L, at : at + L] = jnp.where(later, c1, c0).astype(BF16)
    out[2 * L : 3 * L, at : at + L] = jnp.where(later, c0, 0.0).astype(BF16)


def kernel(
    n_src, n_rcv, scale,
    traces, mask, filters, slots,
    residual, grad_rcv, grad_src,
    xin, mask_in, filt_in, slots_in,
    xt, x3, x3t, floc, send, raw, recv, res, live,
    m128, mt, fm, f_row, table, tabf, taps, g128, gsnd, hrec, toep, x3m,
    gmsg, parts, mine, land_r, land_s, order_r, order_s,
    stage_sems, s_in, s_x, r_x, s_w, r_w, s_f, r_f, s_g, r_g, s_h, r_h, s_p, r_p, s_a, r_a, s_b, r_b,
):
    S, R = lax.axis_index("src"), lax.axis_index("rcv")
    rows_p, cols_q = 2 * n_rcv, 2 * n_src
    rows = n_rcv * 16
    (nl, ny, nc), (nx, nh) = digits_of(n_src, n_rcv)
    l, y, c = S // (ny * nc), lax.rem(S // nc, ny), lax.rem(S, nc)
    x, h = R // nh, lax.rem(R, nh)

    def at_src(dl, dy, dc):
        return (lax.rem(l + dl, nl) * ny + lax.rem(y + dy, ny)) * nc + lax.rem(c + dc, nc)

    def at_rcv(dx, dh):
        return lax.rem(x + dx, nx) * nh + lax.rem(h + dh, nh)

    z = [(at_src(a, 0, 0), at_rcv(0, b)) for a in range(nl) for b in range(nh) if a or b]
    xs = [(S, at_rcv(a, 0)) for a in range(1, nx)]
    ys = [(at_src(0, a, 0), R) for a in range(1, ny)]
    cs = [(at_src(0, 0, a), R) for a in range(1, nc)]
    bar = pltpu.get_barrier_semaphore()
    near = z + xs + ys + cs
    for d in near:
        pl.semaphore_signal(bar, inc=1, device_id=d, device_id_type=MESH)
    loads = [
        pltpu.make_async_copy(a, b, s_in.at[i])
        for i, (a, b) in enumerate(
            ((filters, filt_in), (mask, mask_in), (slots, slots_in), (traces, xin))
        )
    ]
    for a in loads:
        a.start()

    def stage(i, group):
        for d in group:
            pl.semaphore_signal(stage_sems.at[i], inc=1, device_id=d, device_id_type=MESH)

    offsets = rcv_offsets(nx, nh)
    n_raw = raw_of(n_rcv)
    to_rcv = [at_rcv(a, b) for a, b in offsets]
    from_rcv = [at_rcv(nx - a, nh - b) for a, b in offsets[:n_raw]]

    m128[...] = jnp.zeros((L, L), F32)
    fm[...] = jnp.zeros(fm.shape, F32)
    g128[...] = jnp.zeros((L, L), F32)
    gsnd[...] = jnp.zeros(gsnd.shape, F32)
    loads[0].wait()
    f = filt_in[...].astype(F32)
    loads[1].wait()
    m128[0:rows_p, 0:cols_q] = mask_in[...].astype(F32)
    for r in range(n_rcv):
        fm[r, 0:2, :] = f[:, :L]
        fm[r, 2:4, :] = f[:, L:]
        fm[r, 4:6, :] = m128[2 * r : 2 * r + 2, :]

    pl.semaphore_wait(bar, len(near))
    stage(0, xs)
    loads[2].wait()
    loads[3].wait()

    def spread(p, carry):
        for b in range(NB):
            xt[p, pl.ds(b, cols_q, stride=NB), :] = xin[p, :, b * L : (b + 1) * L].astype(F32)
        return carry

    lax.fori_loop(0, rows_p, spread, 0)
    pl.semaphore_wait(stage_sems.at[0], len(xs))

    own8 = pl.ds(pl.multiple_of(R * 8, 8), 8)
    for d in to_rcv[:-1]:
        pltpu.make_async_remote_copy(
            fm.at[d], f_row.at[own8], s_f, r_f, device_id=(S, d), device_id_type=MESH
        ).start()
    stage(1, ys)
    f_row[own8, :] = fm[R]
    for i, d in enumerate(to_rcv[:n_raw]):
        a = xt[2 * d].reshape(n_src, 8, L)
        b = xt[2 * d + 1].reshape(n_src, 8, L)
        raw[i] = swap_middle(a, b)
    mt[...] = jnp.transpose(m128[...])
    pl.semaphore_wait(stage_sems.at[1], len(ys))
    stage(2, cs)
    pl.semaphore_wait(stage_sems.at[2], len(cs))

    for i, d in enumerate(to_rcv[:n_raw]):
        def send_raw(k, carry):
            s = lax.rem(S + k, n_src)
            pltpu.make_async_remote_copy(
                raw.at[i, s], recv.at[S, R], s_w, r_w.at[i], device_id=(s, d), device_id_type=MESH
            ).start()
            return carry

        lax.fori_loop(0, n_src, send_raw, 0)

    wait_bytes(f_row.at[pl.ds(0, (n_rcv - 1) * 8)], r_f)
    for i in range(4):
        table[S, i * n_rcv : (i + 1) * n_rcv, :] = f_row[pl.ds(i, n_rcv, stride=8), :].astype(BF16)

    def send_table(k, carry):
        pltpu.make_async_remote_copy(
            table.at[S], table.at[S], s_g, r_g, device_id=(lax.rem(S + k, n_src), R), device_id_type=MESH
        ).start()
        return carry

    lax.fori_loop(1, n_src, send_table, 0)
    for i in range(2):
        g128[64 + i * n_rcv : 64 + (i + 1) * n_rcv, :] = f_row[pl.ds(4 + i, n_rcv, stride=8), :]
    gt = jnp.transpose(g128[...])
    for s in range(n_src):
        gsnd[s, 0:2, :] = gt[2 * s : 2 * s + 2, :]

    def send_live(k, carry):
        d = lax.rem(S + k, n_src)
        pltpu.make_async_remote_copy(
            gsnd.at[d], hrec.at[S], s_h, r_h, device_id=(d, R), device_id_type=MESH
        ).start()
        return carry

    lax.fori_loop(1, n_src, send_live, 0)
    hrec[S] = gsnd[S]
    flip = jnp.where(iota((L, L), 0) + iota((L, L), 1) == L - 1, 1.0, 0.0).astype(BF16)

    def delays(s, carry):
        v3 = delayed(xt[:, pl.ds(pl.multiple_of(s * 8, 8), 8), :])
        for d in range(3):
            at = (2 - d) * L
            x3[s, :, at : at + L] = v3[d]
            x3t[s, at : at + L, :] = lax.dot_general(
                flip, v3[d], (((1,), (1,)), ((), ())), preferred_element_type=F32
            ).astype(BF16)
        return carry

    lax.fori_loop(0, n_src, delays, 0)

    wait_bytes(table.at[pl.ds(0, n_src - 1)], r_g)
    tabf[...] = table[...].astype(F32).reshape(tabf.shape)

    def pick(slot, w):
        st = slots_in[slot]
        at = (st // (2 * n_rcv)) * (4 * n_rcv) + lax.rem(st, 2) * n_rcv + lax.rem(st // 2, n_rcv)
        taps[pl.ds(2 * w, 1), :] = tabf[pl.ds(at, 1), :]
        taps[pl.ds(2 * w + 1, 1), :] = tabf[pl.ds(at + 2 * n_rcv, 1), :]

    def pick_pair(w, carry):
        slot = (w * n_rcv + R) * 2
        pick(slot, 2 * w)
        pick(slot + 1, 2 * w + 1)
        return carry

    lax.fori_loop(0, n_src, pick_pair, 0)
    for i, d in enumerate(from_rcv):
        for p in range(2):
            pick(S * rows_p + 2 * d + p, cols_q + 2 * i + p)

    later = iota((L, L), 1) >= iota((L, L), 0)
    row8 = iota((rows // 8, 8, L), 1)
    q2 = (row8 // NB).reshape(rows, L)
    p2 = lax.rem(iota((rows, L), 0) // (2 * NB), 2)

    def offset_of(i):
        o = n_src - 1 - i
        return lax.rem(o // nc, nl), o // (nc * nl), lax.rem(o, nc)

    def pair_taps(w, out):
        for i in range(2):
            at = 4 * w + 2 * i
            toeplitz(taps[pl.ds(at, 1), :], taps[pl.ds(at + 1, 1), :], later, out, i * L)

    def filter_two(i0, last):
        to = []
        for u in range(2):
            dl, dy, dc = offset_of(i0 + u)
            s = at_src(dl, dy, dc)
            to.append(s)
            pair_taps(s, toep.at[u])
        for u, s in enumerate(to):
            v = jnp.dot(x3[s], toep[u], preferred_element_type=F32)
            v = jnp.where(q2 == 1, v[:, L:], v[:, :L]).astype(BF16)
            floc[s] = v
            v = v.astype(F32).reshape(n_rcv, 2, 8, L)
            send[s] = swap_middle(v[:, 0], v[:, 1])
        for u, s in enumerate(to):
            own = last and u == 1
            for d in to_rcv[n_raw : n_rcv - (1 if own else 0)]:
                pltpu.make_async_remote_copy(
                    send.at[s, d], recv.at[S, R], s_x, r_x.at[i0 + u], device_id=(s, d), device_id_type=MESH
                ).start()

    def filter_step(i, carry):
        filter_two(2 * i, False)
        return carry

    lax.fori_loop(0, n_src // 2 - 1, filter_step, 0)
    filter_two(n_src - 2, True)
    recv[S, R] = send[S, R]

    for i, d in enumerate(from_rcv):
        wait_bytes(recv.at[0], r_w.at[i])
        v = recv[:, pl.ds(d, 1)].reshape(rows // 8, 8, L).astype(F32)
        v3 = delayed(v)
        for k in range(3):
            x3m[i % 2, :, (2 - k) * L : (3 - k) * L] = v3[k]
        pair_taps(n_src + i, toep.at[i % 2])
        v = jnp.dot(x3m[i % 2], toep[i % 2], preferred_element_type=F32)
        v = jnp.where(p2 == 1, v[:, L:], v[:, :L]).astype(BF16)
        recv[:, pl.ds(d, 1)] = v.reshape(n_src, 1, 16, L)

    wait_bytes(hrec.at[pl.ds(0, n_src - 1)], r_h)
    lane = iota((rows, L), 1)
    tile = iota((rows, L), 0) // 16
    pown = lane == 2 * tile + p2
    prec = lane == 64 + q2 * n_rcv + tile
    ones = jnp.where((iota((L, 2 * L), 0) < 64) == (iota((L, 2 * L), 1) < L), 1.0, 0.0).astype(BF16)

    def widen(i, carry):
        for u in range(2):
            s = 2 * i + u
            own = jnp.where(q2 == 0, mt[pl.ds(2 * s, 1), :], mt[pl.ds(2 * s + 1, 1), :])
            other = jnp.where(p2 == 0, hrec[s, 0:1, :], hrec[s, 1:2, :])
            v = jnp.where(pown, own, jnp.where(prec, other, 0.0)).astype(BF16)
            live[s] = jnp.dot(v, ones, preferred_element_type=F32).astype(BF16)
        return carry

    lax.fori_loop(0, n_src // 2, widen, 0)

    reach = iota((L, L), 1) + iota((L, L), 0) >= L - 1

    def lag_pairs(i0, count, last):
        found = []
        for u in range(count):
            dl, dy, dc = offset_of(i0 + u)
            s = at_src(nl - dl, ny - dy, nc - dc)
            wait_bytes(recv.at[0, pl.ds(0, n_rcv - n_raw - (1 if last else 0))], r_x.at[i0 + u])
            found.append(s)
        ms = []
        for s in found:
            diff = floc[s].astype(F32) - recv[s].reshape(rows, L).astype(F32)
            lv = live[s].astype(F32)
            for t in range(2):
                r = lv[:, t * L : (t + 1) * L] * diff
                if t == 0:
                    res[:, pl.ds(pl.multiple_of(s * 8, 8), 8), :] = r.reshape(rows_p, 8, L)
                both = jnp.concatenate([jnp.where(q2 == 0, r, 0.0), jnp.where(q2 == 1, r, 0.0)], axis=1)
                ms.append(jnp.dot(x3t[s], both.astype(BF16), preferred_element_type=F32))
        for u, s in enumerate(found):
            sums = []
            for t in range(2):
                m = ms[2 * u + t]
                for i in range(2):
                    mi = m[:, i * L : (i + 1) * L]
                    m2, m1, m0 = mi[0:L], mi[L : 2 * L], mi[2 * L : 3 * L]
                    for a, b in ((m0, m1), (m1, m2)):
                        skew = pltpu.roll(jnp.where(reach, a, b), 1, 1, stride=1, stride_axis=0)
                        sums.append(jnp.sum(skew, axis=0, keepdims=True))
            msg = jnp.concatenate(sums, axis=0)
            if last:
                parts[S] = msg
            else:
                gmsg[s] = msg
                pltpu.make_async_remote_copy(
                    gmsg.at[s], parts.at[S], s_p, r_p, device_id=(s, R), device_id_type=MESH
                ).start()

    def lag_step(i, carry):
        lag_pairs(2 * i, 2, False)
        return carry

    lax.fori_loop(0, n_src // 2 - 1, lag_step, 0)
    lag_pairs(n_src - 2, 1, False)
    lag_pairs(n_src - 1, 1, True)

    wait_bytes(parts.at[pl.ds(0, n_src - 1)], r_p)
    total = jnp.sum(parts[...], axis=0) * scale
    mine[0] = total[:4]
    mine[1] = total[4:]
    for d in to_rcv[:-1]:
        pltpu.make_async_remote_copy(
            mine.at[1], land_s.at[R], s_b, r_b, device_id=(S, d), device_id_type=MESH
        ).start()

    def send_src(k, carry):
        pltpu.make_async_remote_copy(
            mine.at[0], land_r.at[S], s_a, r_a, device_id=(lax.rem(S + k, n_src), R), device_id_type=MESH
        ).start()
        return carry

    lax.fori_loop(1, n_src, send_src, 0)
    land_r[S] = total[:4]
    land_s[R] = total[4:]

    def gather(p, carry):
        for b in range(NB):
            residual[p, :, b * L : (b + 1) * L] = res[p, pl.ds(b, cols_q, stride=NB), :].astype(BF16)
        return carry

    lax.fori_loop(0, rows_p, gather, 0)
    wait_bytes(f_row.at[pl.ds(0, (n_rcv - 1) * 8)], s_f)
    wait_bytes(table.at[pl.ds(0, n_src - 1)], s_g)
    wait_bytes(hrec.at[pl.ds(0, n_src - 1)], s_h)
    wait_bytes(parts.at[pl.ds(0, n_src - 1)], s_p)
    wait_bytes(raw, s_w)
    for i in range(n_src):
        wait_bytes(recv.at[0, pl.ds(0, n_rcv - n_raw - (1 if i == n_src - 1 else 0))], s_x)
    wait_bytes(land_r.at[pl.ds(0, n_src - 1)], s_a)
    wait_bytes(land_s.at[pl.ds(0, n_rcv - 1)], s_b)
    wait_bytes(land_r.at[pl.ds(0, n_src - 1)], r_a)
    wait_bytes(land_s.at[pl.ds(0, n_rcv - 1)], r_b)
    for i in range(2):
        for k in range(2):
            order_r[k, pl.ds(i, n_src, stride=2), :] = land_r[:, 2 * i + k, :]
            order_s[k, pl.ds(i, n_rcv, stride=2), :] = land_s[:, 2 * i + k, :]
    for k in range(2):
        at = slice(k * L, (k + 1) * L)
        grad_rcv[:, at] = order_r[k]
        grad_src[:, at] = order_s[k]


def shards(traces, dead_mask, filters, station_of_slot):
    rows_p, cols_q, trace_len = traces.shape
    tap_count = filters.shape[1]
    n_src, n_rcv = lax.axis_size("src"), lax.axis_size("rcv")
    rows = n_rcv * 16
    n_raw = raw_of(n_rcv)
    scale = 1.0 / math.sqrt(rows_p * n_src * trace_len)
    vm = pl.BlockSpec(memory_space=pltpu.VMEM)
    hbm = pl.BlockSpec(memory_space=pltpu.HBM)
    V = pltpu.VMEM
    D = pltpu.SemaphoreType.DMA
    shapes = (
        jax.ShapeDtypeStruct(traces.shape, BF16),
        jax.ShapeDtypeStruct((cols_q, tap_count), F32),
        jax.ShapeDtypeStruct((rows_p, tap_count), F32),
    )
    outs = pl.pallas_call(
        functools.partial(kernel, n_src, n_rcv, scale),
        out_shape=shapes,
        in_specs=[hbm] * 4,
        out_specs=(vm, vm, vm),
        scratch_shapes=[
            V(traces.shape, BF16),
            V(dead_mask.shape, jnp.int32),
            V(filters.shape, BF16),
            pltpu.SMEM(station_of_slot.shape, jnp.int32),
            V((rows_p, NB * cols_q, L), F32),
            V((n_src, rows, 3 * L), BF16),
            V((n_src, 3 * L, rows), BF16),
            V((n_src, rows, L), BF16),
            V((n_src, n_rcv, 16, L), BF16),
            V((n_raw, n_src, 16, L), BF16),
            V((n_src, n_rcv, 16, L), BF16),
            V((rows_p, NB * cols_q, L), F32),
            V((n_src, rows, 2 * L), BF16),
            V((L, L), F32),
            V((L, L), F32),
            V((n_rcv, 8, L), F32),
            V((n_rcv * 8, L), F32),
            V((n_src, 4 * n_rcv, L), BF16),
            V((n_src * 4 * n_rcv, L), F32),
            V((2 * cols_q + 4 * n_raw, L), F32),
            V((L, L), F32),
            V((n_src, 8, L), F32),
            V((n_src, 8, L), F32),
            V((2, 3 * L, 2 * L), BF16),
            V((2, rows, 3 * L), BF16),
            V((n_src, 8, L), F32),
            V((n_src, 8, L), F32),
            V((2, 4, L), F32),
            V((n_src, 4, L), F32),
            V((n_rcv, 4, L), F32),
            V((2, cols_q, L), F32),
            V((2, rows_p, L), F32),
            pltpu.SemaphoreType.REGULAR((3,)),
            D((4,)), D, D((n_src,)), D, D((n_raw,)),
            D, D, D, D, D, D, D, D, D, D, D, D,
        ],
        compiler_params=pltpu.CompilerParams(
            collective_id=0, has_side_effects=True, vmem_limit_bytes=60 << 20
        ),
    )(traces, dead_mask, filters, station_of_slot)
    return outs


def solution(mesh):
    placed = (P("src", "rcv", None), P("src", "rcv"), P(("src", "rcv"), None), P())
    return jax.shard_map(
        shards,
        mesh=mesh,
        in_specs=placed,
        out_specs=(P("src", "rcv", None), P("rcv", None), P("src", None)),
        check_vma=False,
    )
```

time: 70.2 us -> 60.4 us (0.86)
  Pallas kernels: 63.8 us -> 55.9 us
  local copies, waits for them, and re-layouts: 5.53 us -> 3.7 us
    pallas_call x1, Pallas kernels: 63.8 us -> 55.9 us  [shards(): pl.pallas_call(functools.partial(kernel, n_src, n_rcv, scale), out_shape=...]
    reshape x2 -> x0, local copies, waits for them, and re-layouts: 1.27 us -> none  [the longest x1 0.63 us: shards(): grad_rcv.reshape(cols_q, tap_count)]
    unnamed x9 -> x7, local copies, waits for them, and re-layouts: 4.26 us -> 3.7 us
where the time goes in v3:
time: 60.4 us; the launch traced here: 60.2 us
  Pallas kernels  55.9 us (93%)
  local copies, waits for them, and re-layouts  3.7 us (6%)
  between operations  0.65 us (1%)
    pallas_call x1, Pallas kernels, shards(): pl.pallas_call(functools.partial(kernel, n_src, n_rcv, scale), out_shape=...  55.9 us
    unnamed x7, local copies, waits for them, and re-layouts  3.7 us

profile of v3, /device:TPU:1, one launch (start us, length us, event | category | flops | bytes accessed | tf_op | source)
XLA Modules:
  0.0 60.2 jit_solution(17953923979894144636)
XLA Ops:
  0.6 55.9 %shard_map.67 = (bf16[32,32,512]{2,1,0:T(8,128)(2,1)}, f32[32,256]{1,0:T(8,128)}, f32[32,256]{1,0:T(8,128)}) custom-call(bf16[32,32,512]{2,1,0:T(8,128)(2,1)} %traces.1, s32[32,32]{1,0:T(8,128)} %mask.1, bf16[2,256]{1,0:T(2,128)(2,1)} %filters.1, s32[512]{0:T(512)} %slots.1), custom_call_target="tpu_custom_call" | custom-call | tf_op jit(solution)/shard_map/pallas_call | solution.py:408
  56.5 0.0 copy-start.1
  56.5 2.3 %copy.10 = bf16[32,32,512]{2,1,0:T(8,128)(2,1)} copy(bf16[32,32,512]{2,1,0:T(8,128)(2,1)} %get-tuple-element.6) | data formatting | bytes 2097152
  58.9 0.0 copy-done.1
  58.9 0.0 copy-start
  58.9 0.6 %copy.11 = f32[32,256]{1,0:T(8,128)} copy(f32[32,256]{1,0:T(8,128)S(1)} %copy-done.1) | data formatting | bytes 65536
  59.5 0.2 copy-done
  59.6 0.6 %copy.12 = f32[32,256]{1,0:T(8,128)} copy(f32[32,256]{1,0:T(8,128)S(1)} %copy-done) | data formatting | bytes 65536
Async XLA Ops:
  56.5 2.3 %copy-start.1 = (f32[32,256]{1,0:T(8,128)S(1)}, f32[32,256]{1,0:T(8,128)}, u32[]{:S(2)}) copy-start(f32[32,256]{1,0:T(8,128)} %get-tuple-element.7) | copy-start | bytes 98308
  58.9 0.8 %copy-start = (f32[32,256]{1,0:T(8,128)S(1)}, f32[32,256]{1,0:T(8,128)}, u32[]{:S(2)}) copy-start(f32[32,256]{1,0:T(8,128)} %get-tuple-element.8) | copy-start | bytes 98308

commit v4 on v3

--- a/solution.py
+++ b/solution.py
@@ -13,7 +13,8 @@
 BF16 = jnp.bfloat16
 NB = 4
 L = 128
-RAW = 4
+RAW = 8
+AHEAD = 2
 
 
 def digits_of(n_src, n_rcv):
@@ -73,7 +74,7 @@
     xt, x3, x3t, floc, send, raw, recv, res, live,
     m128, mt, fm, f_row, table, tabf, taps, g128, gsnd, hrec, toep, x3m,
     gmsg, parts, mine, land_r, land_s, order_r, order_s,
-    stage_sems, s_in, s_x, r_x, s_w, r_w, s_f, r_f, s_g, r_g, s_h, r_h, s_p, r_p, s_a, r_a, s_b, r_b,
+    stage_sems, s_in, s_x, r_x, s_w, r_w, s_f, r_f, s_g, r_g, s_z, r_z, s_h, r_h, s_p, r_p, s_a, r_a, s_b, r_b,
 ):
     S, R = lax.axis_index("src"), lax.axis_index("rcv")
     rows_p, cols_q = 2 * n_rcv, 2 * n_src
@@ -117,7 +118,6 @@
     m128[...] = jnp.zeros((L, L), F32)
     fm[...] = jnp.zeros(fm.shape, F32)
     g128[...] = jnp.zeros((L, L), F32)
-    gsnd[...] = jnp.zeros(gsnd.shape, F32)
     loads[0].wait()
     f = filt_in[...].astype(F32)
     loads[1].wait()
@@ -156,32 +156,34 @@
     stage(2, cs)
     pl.semaphore_wait(stage_sems.at[2], len(cs))
 
-    for i, d in enumerate(to_rcv[:n_raw]):
-        def send_raw(k, carry):
-            s = lax.rem(S + k, n_src)
-            pltpu.make_async_remote_copy(
-                raw.at[i, s], recv.at[S, R], s_w, r_w.at[i], device_id=(s, d), device_id_type=MESH
-            ).start()
-            return carry
-
-        lax.fori_loop(0, n_src, send_raw, 0)
+    def send_raw(group):
+        for i in group:
+            def step(k, carry):
+                s = lax.rem(S + k, n_src)
+                pltpu.make_async_remote_copy(
+                    raw.at[i, s], recv.at[S, R], s_w, r_w.at[i], device_id=(s, to_rcv[i]), device_id_type=MESH
+                ).start()
+                return carry
+
+            lax.fori_loop(0, n_src, step, 0)
+
+    n_ahead = min(AHEAD, n_raw)
+    send_raw(range(n_ahead))
 
     wait_bytes(f_row.at[pl.ds(0, (n_rcv - 1) * 8)], r_f)
     for i in range(4):
         table[S, i * n_rcv : (i + 1) * n_rcv, :] = f_row[pl.ds(i, n_rcv, stride=8), :].astype(BF16)
 
-    def send_table(k, carry):
+    lines = [at_src(a, 0, 0) for a in range(nl)]
+    for d in lines[1:]:
         pltpu.make_async_remote_copy(
-            table.at[S], table.at[S], s_g, r_g, device_id=(lax.rem(S + k, n_src), R), device_id_type=MESH
+            table.at[S], table.at[S], s_z, r_z, device_id=(d, R), device_id_type=MESH
         ).start()
-        return carry
-
-    lax.fori_loop(1, n_src, send_table, 0)
     for i in range(2):
         g128[64 + i * n_rcv : 64 + (i + 1) * n_rcv, :] = f_row[pl.ds(4 + i, n_rcv, stride=8), :]
     gt = jnp.transpose(g128[...])
     for s in range(n_src):
-        gsnd[s, 0:2, :] = gt[2 * s : 2 * s + 2, :]
+        gsnd[s] = gt[2 * s : 2 * s + 2, :]
 
     def send_live(k, carry):
         d = lax.rem(S + k, n_src)
@@ -191,6 +193,8 @@
         return carry
 
     lax.fori_loop(1, n_src, send_live, 0)
+
+    send_raw(range(n_ahead, n_raw))
     hrec[S] = gsnd[S]
     flip = jnp.where(iota((L, L), 0) + iota((L, L), 1) == L - 1, 1.0, 0.0).astype(BF16)
 
@@ -206,7 +210,17 @@
 
     lax.fori_loop(0, n_src, delays, 0)
 
-    wait_bytes(table.at[pl.ds(0, n_src - 1)], r_g)
+    if nl > 1:
+        wait_bytes(table.at[pl.ds(0, nl - 1)], r_z)
+    for a in range(1, ny * nc):
+        d = at_src(0, a // nc, a % nc)
+        for b in lines:
+            pltpu.make_async_remote_copy(
+                table.at[b], table.at[b], s_g, r_g, device_id=(d, R), device_id_type=MESH
+            ).start()
+    if nl > 1:
+        wait_bytes(table.at[pl.ds(0, nl - 1)], s_z)
+    wait_bytes(table.at[pl.ds(0, n_src - nl)], r_g)
     tabf[...] = table[...].astype(F32).reshape(tabf.shape)
 
     def pick(slot, w):
@@ -369,7 +383,7 @@
 
     lax.fori_loop(0, rows_p, gather, 0)
     wait_bytes(f_row.at[pl.ds(0, (n_rcv - 1) * 8)], s_f)
-    wait_bytes(table.at[pl.ds(0, n_src - 1)], s_g)
+    wait_bytes(table.at[pl.ds(0, n_src - nl)], s_g)
     wait_bytes(hrec.at[pl.ds(0, n_src - 1)], s_h)
     wait_bytes(parts.at[pl.ds(0, n_src - 1)], s_p)
     wait_bytes(raw, s_w)
@@ -387,6 +401,12 @@
         at = slice(k * L, (k + 1) * L)
         grad_rcv[:, at] = order_r[k]
         grad_src[:, at] = order_s[k]
+
+
+def hand_on(a, b, c, x, y, z):
+    x[...] = a[...]
+    y[...] = b[...]
+    z[...] = c[...]
 
 
 def shards(traces, dead_mask, filters, station_of_slot):
@@ -432,8 +452,8 @@
             V((n_src * 4 * n_rcv, L), F32),
             V((2 * cols_q + 4 * n_raw, L), F32),
             V((L, L), F32),
-            V((n_src, 8, L), F32),
-            V((n_src, 8, L), F32),
+            V((n_src, 2, L), F32),
+            V((n_src, 2, L), F32),
             V((2, 3 * L, 2 * L), BF16),
             V((2, rows, 3 * L), BF16),
             V((n_src, 8, L), F32),
@@ -445,13 +465,15 @@
             V((2, rows_p, L), F32),
             pltpu.SemaphoreType.REGULAR((3,)),
             D((4,)), D, D((n_src,)), D, D((n_raw,)),
-            D, D, D, D, D, D, D, D, D, D, D, D,
+            D, D, D, D, D, D, D, D, D, D, D, D, D, D,
         ],
         compiler_params=pltpu.CompilerParams(
             collective_id=0, has_side_effects=True, vmem_limit_bytes=60 << 20
         ),
     )(traces, dead_mask, filters, station_of_slot)
-    return outs
+    return pl.pallas_call(
+        hand_on, out_shape=shapes, in_specs=[vm] * 3, out_specs=(vm,) * 3
+    )(*outs)
 
 
 def solution(mesh):

time: 60.4 us -> 55.9 us (0.925)
  local copies, waits for them, and re-layouts: 3.7 us -> 0 us
  Pallas kernels: 55.9 us -> 55.1 us
    unnamed x7 -> x0, local copies, waits for them, and re-layouts: 3.7 us -> none
    pallas_call x1, Pallas kernels: 55.9 us -> 52.8 us  [shards(): pl.pallas_call(functools.partial(kernel, n_src, n_rcv, scale), out_shape=...]
    pallas_call x0 -> x1, Pallas kernels: none -> 2.29 us  [shards(): pl.pallas_call(hand_on, out_shape=shapes, in_specs=[vm] * 3, out_specs=(v...]
where the time goes in v4:
time: 55.9 us; the launch traced here: 55.7 us
  Pallas kernels  55.1 us (99%)
  between operations  0.64 us (1%)
    pallas_call x1, Pallas kernels, shards(): pl.pallas_call(functools.partial(kernel, n_src, n_rcv, scale), out_shape=...  52.8 us
    pallas_call x1, Pallas kernels, shards(): pl.pallas_call(hand_on, out_shape=shapes, in_specs=[vm] * 3, out_specs=(v...  2.29 us

profile of v4, /device:TPU:1, one launch (start us, length us, event | category | flops | bytes accessed | tf_op | source)
XLA Modules:
  0.0 55.7 jit_solution(1788194227264882112)
XLA Ops:
  0.6 52.8 %shard_map.67 = (bf16[32,32,512]{2,1,0:T(8,128)(2,1)}, f32[32,256]{1,0:T(8,128)}, f32[32,256]{1,0:T(8,128)}) custom-call(bf16[32,32,512]{2,1,0:T(8,128)(2,1)} %traces.1, s32[32,32]{1,0:T(8,128)} %mask.1, bf16[2,256]{1,0:T(2,128)(2,1)} %filters.1, s32[512]{0:T(512)} %slots.1), custom_call_target="tpu_custom_call" | custom-call | tf_op jit(solution)/shard_map/pallas_call | solution.py:428
  53.5 2.3 %shard_map.68 = (bf16[32,32,512]{2,1,0:T(8,128)(2,1)}, f32[32,256]{1,0:T(8,128)}, f32[32,256]{1,0:T(8,128)}) custom-call(bf16[32,32,512]{2,1,0:T(8,128)(2,1)} %get-tuple-element.6.a, f32[32,256]{1,0:T(8,128)} %get-tuple-element.7.b, f32[32,256]{1,0:T(8,128)} %get-tuple-element.8.c), custom_call_target="tpu_custom_call" | custom-call | tf_op jit(solution)/shard_map/pallas_call | solution.py:474

commit v5 on v4

--- a/solution.py
+++ b/solution.py
@@ -13,8 +13,8 @@
 BF16 = jnp.bfloat16
 NB = 4
 L = 128
-RAW = 8
-AHEAD = 2
+RAW = 6
+AHEAD = 3
 
 
 def digits_of(n_src, n_rcv):
@@ -74,7 +74,7 @@
     xt, x3, x3t, floc, send, raw, recv, res, live,
     m128, mt, fm, f_row, table, tabf, taps, g128, gsnd, hrec, toep, x3m,
     gmsg, parts, mine, land_r, land_s, order_r, order_s,
-    stage_sems, s_in, s_x, r_x, s_w, r_w, s_f, r_f, s_g, r_g, s_z, r_z, s_h, r_h, s_p, r_p, s_a, r_a, s_b, r_b,
+    stage_sems, s_in, s_x, r_x, s_w, r_w, s_f, r_f, s_g, r_g, s_z, r_z, s_c, r_c, s_h, r_h, s_p, r_p, s_a, r_a, s_b, r_b,
 ):
     S, R = lax.axis_index("src"), lax.axis_index("rcv")
     rows_p, cols_q = 2 * n_rcv, 2 * n_src
@@ -212,15 +212,22 @@
 
     if nl > 1:
         wait_bytes(table.at[pl.ds(0, nl - 1)], r_z)
-    for a in range(1, ny * nc):
-        d = at_src(0, a // nc, a % nc)
+    for a in range(1, ny):
         for b in lines:
             pltpu.make_async_remote_copy(
-                table.at[b], table.at[b], s_g, r_g, device_id=(d, R), device_id_type=MESH
+                table.at[b], table.at[b], s_g, r_g, device_id=(at_src(0, a, 0), R), device_id_type=MESH
             ).start()
     if nl > 1:
         wait_bytes(table.at[pl.ds(0, nl - 1)], s_z)
-    wait_bytes(table.at[pl.ds(0, n_src - nl)], r_g)
+    wait_bytes(table.at[pl.ds(0, nl * (ny - 1))], r_g)
+    for k in range(1, nc):
+        for a in range(nl):
+            for b in range(ny):
+                t = at_src(a, b, 0)
+                pltpu.make_async_remote_copy(
+                    table.at[t], table.at[t], s_c, r_c, device_id=(at_src(0, 0, k), R), device_id_type=MESH
+                ).start()
+    wait_bytes(table.at[pl.ds(0, n_src - nl * ny)], r_c)
     tabf[...] = table[...].astype(F32).reshape(tabf.shape)
 
     def pick(slot, w):
@@ -378,12 +385,15 @@
 
     def gather(p, carry):
         for b in range(NB):
-            residual[p, :, b * L : (b + 1) * L] = res[p, pl.ds(b, cols_q, stride=NB), :].astype(BF16)
+            xin[p, :, b * L : (b + 1) * L] = res[p, pl.ds(b, cols_q, stride=NB), :].astype(BF16)
         return carry
 
     lax.fori_loop(0, rows_p, gather, 0)
+    store = pltpu.make_async_copy(xin, residual, s_in.at[3])
+    store.start()
     wait_bytes(f_row.at[pl.ds(0, (n_rcv - 1) * 8)], s_f)
-    wait_bytes(table.at[pl.ds(0, n_src - nl)], s_g)
+    wait_bytes(table.at[pl.ds(0, nl * (ny - 1))], s_g)
+    wait_bytes(table.at[pl.ds(0, n_src - nl * ny)], s_c)
     wait_bytes(hrec.at[pl.ds(0, n_src - 1)], s_h)
     wait_bytes(parts.at[pl.ds(0, n_src - 1)], s_p)
     wait_bytes(raw, s_w)
@@ -401,12 +411,22 @@
         at = slice(k * L, (k + 1) * L)
         grad_rcv[:, at] = order_r[k]
         grad_src[:, at] = order_s[k]
-
-
-def hand_on(a, b, c, x, y, z):
-    x[...] = a[...]
-    y[...] = b[...]
-    z[...] = c[...]
+    store.wait()
+
+
+def hand_on(a, b, c, x, y, z, buf, buf_r, buf_s, sems):
+    parts = buf.shape[0] // 4
+    ways = [(a.at[pl.ds(i * parts, parts)], buf.at[pl.ds(i * parts, parts)], x.at[pl.ds(i * parts, parts)]) for i in range(4)]
+    ways += [(b, buf_r, y), (c, buf_s, z)]
+    loads = [pltpu.make_async_copy(i, m, sems.at[0, k]) for k, (i, m, o) in enumerate(ways)]
+    stores = [pltpu.make_async_copy(m, o, sems.at[1, k]) for k, (i, m, o) in enumerate(ways)]
+    for copy in loads:
+        copy.start()
+    for load, store in zip(loads, stores):
+        load.wait()
+        store.start()
+    for copy in stores:
+        copy.wait()
 
 
 def shards(traces, dead_mask, filters, station_of_slot):
@@ -429,7 +449,7 @@
         functools.partial(kernel, n_src, n_rcv, scale),
         out_shape=shapes,
         in_specs=[hbm] * 4,
-        out_specs=(vm, vm, vm),
+        out_specs=(hbm, vm, vm),
         scratch_shapes=[
             V(traces.shape, BF16),
             V(dead_mask.shape, jnp.int32),
@@ -465,14 +485,18 @@
             V((2, rows_p, L), F32),
             pltpu.SemaphoreType.REGULAR((3,)),
             D((4,)), D, D((n_src,)), D, D((n_raw,)),
-            D, D, D, D, D, D, D, D, D, D, D, D, D, D,
+            D, D, D, D, D, D, D, D, D, D, D, D, D, D, D, D,
         ],
         compiler_params=pltpu.CompilerParams(
             collective_id=0, has_side_effects=True, vmem_limit_bytes=60 << 20
         ),
     )(traces, dead_mask, filters, station_of_slot)
     return pl.pallas_call(
-        hand_on, out_shape=shapes, in_specs=[vm] * 3, out_specs=(vm,) * 3
+        hand_on,
+        out_shape=shapes,
+        in_specs=[hbm] * 3,
+        out_specs=(hbm,) * 3,
+        scratch_shapes=[V(traces.shape, BF16), V(shapes[1].shape, F32), V(shapes[2].shape, F32), D((2, 6))],
     )(*outs)
 
 

time: 55.9 us -> 55.2 us (0.987)
  Pallas kernels: 55.1 us -> 54.5 us
where the time goes in v5:
time: 55.2 us; the launch traced here: 55.1 us
  Pallas kernels  54.5 us (99%)
  between operations  0.64 us (1%)
    pallas_call x1, Pallas kernels, shards(): pl.pallas_call(functools.partial(kernel, n_src, n_rcv, scale), out_shape=...  52.4 us
    pallas_call x1, Pallas kernels, shards(): pl.pallas_call(hand_on, out_shape=shapes, in_specs=[hbm] * 3, out_specs=(...  2.03 us

profile of v5, /device:TPU:1, one launch (start us, length us, event | category | flops | bytes accessed | tf_op | source)
XLA Modules:
  0.0 55.1 jit_solution(798195125114802354)
XLA Ops:
  0.6 52.4 %shard_map.67 = (bf16[32,32,512]{2,1,0:T(8,128)(2,1)}, f32[32,256]{1,0:T(8,128)}, f32[32,256]{1,0:T(8,128)}) custom-call(bf16[32,32,512]{2,1,0:T(8,128)(2,1)} %traces.1, s32[32,32]{1,0:T(8,128)} %mask.1, bf16[2,256]{1,0:T(2,128)(2,1)} %filters.1, s32[512]{0:T(512)} %slots.1), custom_call_target="tpu_custom_call" | custom-call | tf_op jit(solution)/shard_map/pallas_call | solution.py:448
  53.1 2.0 %shard_map.68 = (bf16[32,32,512]{2,1,0:T(8,128)(2,1)}, f32[32,256]{1,0:T(8,128)}, f32[32,256]{1,0:T(8,128)}) custom-call(bf16[32,32,512]{2,1,0:T(8,128)(2,1)} %get-tuple-element.6.a, f32[32,256]{1,0:T(8,128)} %get-tuple-element.7.b, f32[32,256]{1,0:T(8,128)} %get-tuple-element.8.c), custom_call_target="tpu_custom_call" | custom-call | tf_op jit(solution)/shard_map/pallas_call | solution.py:494

commit v6 on v5

--- a/solution.py
+++ b/solution.py
@@ -13,7 +13,7 @@
 BF16 = jnp.bfloat16
 NB = 4
 L = 128
-RAW = 6
+RAW = 7
 AHEAD = 3
 
 
@@ -289,6 +289,24 @@
     filter_two(n_src - 2, True)
     recv[S, R] = send[S, R]
 
+    wait_bytes(hrec.at[pl.ds(0, n_src - 1)], r_h)
+    lane = iota((rows, L), 1)
+    tile = iota((rows, L), 0) // 16
+    pown = lane == 2 * tile + p2
+    prec = lane == 64 + q2 * n_rcv + tile
+    ones = jnp.where((iota((L, 2 * L), 0) < 64) == (iota((L, 2 * L), 1) < L), 1.0, 0.0).astype(BF16)
+
+    def widen(i, carry):
+        for u in range(2):
+            s = 2 * i + u
+            own = jnp.where(q2 == 0, mt[pl.ds(2 * s, 1), :], mt[pl.ds(2 * s + 1, 1), :])
+            other = jnp.where(p2 == 0, hrec[s, 0:1, :], hrec[s, 1:2, :])
+            v = jnp.where(pown, own, jnp.where(prec, other, 0.0)).astype(BF16)
+            live[s] = jnp.dot(v, ones, preferred_element_type=F32).astype(BF16)
+        return carry
+
+    lax.fori_loop(0, n_src // 2, widen, 0)
+
     for i, d in enumerate(from_rcv):
         wait_bytes(recv.at[0], r_w.at[i])
         v = recv[:, pl.ds(d, 1)].reshape(rows // 8, 8, L).astype(F32)
@@ -299,24 +317,6 @@
         v = jnp.dot(x3m[i % 2], toep[i % 2], preferred_element_type=F32)
         v = jnp.where(p2 == 1, v[:, L:], v[:, :L]).astype(BF16)
         recv[:, pl.ds(d, 1)] = v.reshape(n_src, 1, 16, L)
-
-    wait_bytes(hrec.at[pl.ds(0, n_src - 1)], r_h)
-    lane = iota((rows, L), 1)
-    tile = iota((rows, L), 0) // 16
-    pown = lane == 2 * tile + p2
-    prec = lane == 64 + q2 * n_rcv + tile
-    ones = jnp.where((iota((L, 2 * L), 0) < 64) == (iota((L, 2 * L), 1) < L), 1.0, 0.0).astype(BF16)
-
-    def widen(i, carry):
-        for u in range(2):
-            s = 2 * i + u
-            own = jnp.where(q2 == 0, mt[pl.ds(2 * s, 1), :], mt[pl.ds(2 * s + 1, 1), :])
-            other = jnp.where(p2 == 0, hrec[s, 0:1, :], hrec[s, 1:2, :])
-            v = jnp.where(pown, own, jnp.where(prec, other, 0.0)).astype(BF16)
-            live[s] = jnp.dot(v, ones, preferred_element_type=F32).astype(BF16)
-        return carry
-
-    lax.fori_loop(0, n_src // 2, widen, 0)
 
     reach = iota((L, L), 1) + iota((L, L), 0) >= L - 1
 

time: 55.2 us -> 54.9 us (level)
  no operation moved by 1% of the time
where the time goes in v6:
time: 54.9 us; the launch traced here: 54.8 us
  Pallas kernels  54.1 us (99%)
  between operations  0.64 us (1%)
    pallas_call x1, Pallas kernels, shards(): pl.pallas_call(functools.partial(kernel, n_src, n_rcv, scale), out_shape=...  52.1 us
    pallas_call x1, Pallas kernels, shards(): pl.pallas_call(hand_on, out_shape=shapes, in_specs=[hbm] * 3, out_specs=(...  2.03 us

profile of v6, /device:TPU:1, one launch (start us, length us, event | category | flops | bytes accessed | tf_op | source)
XLA Modules:
  0.0 54.8 jit_solution(9379479441676851162)
XLA Ops:
  0.6 52.1 %shard_map.67 = (bf16[32,32,512]{2,1,0:T(8,128)(2,1)}, f32[32,256]{1,0:T(8,128)}, f32[32,256]{1,0:T(8,128)}) custom-call(bf16[32,32,512]{2,1,0:T(8,128)(2,1)} %traces.1, s32[32,32]{1,0:T(8,128)} %mask.1, bf16[2,256]{1,0:T(2,128)(2,1)} %filters.1, s32[512]{0:T(512)} %slots.1), custom_call_target="tpu_custom_call" | custom-call | tf_op jit(solution)/shard_map/pallas_call | solution.py:448
  52.8 2.0 %shard_map.68 = (bf16[32,32,512]{2,1,0:T(8,128)(2,1)}, f32[32,256]{1,0:T(8,128)}, f32[32,256]{1,0:T(8,128)}) custom-call(bf16[32,32,512]{2,1,0:T(8,128)(2,1)} %get-tuple-element.6.a, f32[32,256]{1,0:T(8,128)} %get-tuple-element.7.b, f32[32,256]{1,0:T(8,128)} %get-tuple-element.8.c), custom_call_target="tpu_custom_call" | custom-call | tf_op jit(solution)/shard_map/pallas_call | solution.py:494

commit v7 on v6

--- a/solution.py
+++ b/solution.py
@@ -14,7 +14,7 @@
 NB = 4
 L = 128
 RAW = 7
-AHEAD = 3
+AHEAD = 4
 
 
 def digits_of(n_src, n_rcv):

time: 54.9 us -> 55.4 us (level)
  no operation moved by 1% of the time
where the time goes in v7:
time: 55.4 us; the launch traced here: 55.3 us
  Pallas kernels  54.6 us (99%)
  between operations  0.64 us (1%)
    pallas_call x1, Pallas kernels, shards(): pl.pallas_call(functools.partial(kernel, n_src, n_rcv, scale), out_shape=...  52.6 us
    pallas_call x1, Pallas kernels, shards(): pl.pallas_call(hand_on, out_shape=shapes, in_specs=[hbm] * 3, out_specs=(...  2.03 us

profile of v7, /device:TPU:1, one launch (start us, length us, event | category | flops | bytes accessed | tf_op | source)
XLA Modules:
  0.0 55.3 jit_solution(4550551853231320433)
XLA Ops:
  0.6 52.6 %shard_map.67 = (bf16[32,32,512]{2,1,0:T(8,128)(2,1)}, f32[32,256]{1,0:T(8,128)}, f32[32,256]{1,0:T(8,128)}) custom-call(bf16[32,32,512]{2,1,0:T(8,128)(2,1)} %traces.1, s32[32,32]{1,0:T(8,128)} %mask.1, bf16[2,256]{1,0:T(2,128)(2,1)} %filters.1, s32[512]{0:T(512)} %slots.1), custom_call_target="tpu_custom_call" | custom-call | tf_op jit(solution)/shard_map/pallas_call | solution.py:448
  53.2 2.0 %shard_map.68 = (bf16[32,32,512]{2,1,0:T(8,128)(2,1)}, f32[32,256]{1,0:T(8,128)}, f32[32,256]{1,0:T(8,128)}) custom-call(bf16[32,32,512]{2,1,0:T(8,128)(2,1)} %get-tuple-element.6.a, f32[32,256]{1,0:T(8,128)} %get-tuple-element.7.b, f32[32,256]{1,0:T(8,128)} %get-tuple-element.8.c), custom_call_target="tpu_custom_call" | custom-call | tf_op jit(solution)/shard_map/pallas_call | solution.py:494
